TPU v7x, 128 devices: a whole 4x4x4 slice. The times are simulated.
128 devices in a mesh: seq: 16 (over y, x), tp: 8 (over z, core).
Axes of the slice: x: 4, y: 4, z: 4, core: 2. Of those that a mesh axis runs over, the one named last changes fastest.
Arguments:
- hidden: bfloat16 [8192, 4096], P('seq', 'tp'), may hold values from -6 to 6
- norm_gain: bfloat16 [4096], replicated, may hold values from 0.25 to 1.75
- gate_x_weight: bfloat16 [4096, 2, 4096], P(None, None, 'tp'), may hold values from -0.09375 to 0.09375
- state_weight: bfloat16 [4096, 2, 1024], P(None, None, 'tp'), may hold values from -0.09375 to 0.09375
- step_weight: bfloat16 [4096, 64], P(None, 'tp'), may hold values from -0.09375 to 0.09375
- conv_inner: bfloat16 [4, 4096], P(None, 'tp'), may hold values from -0.75 to 0.75
- conv_state: bfloat16 [4, 2, 1024], P(None, None, 'tp'), may hold values from -0.75 to 0.75
- step_bias: float32 [64], P('tp'), may hold values from -6 to -1.5
- decay_log: float32 [64], P('tp'), may hold values from -12 to 1
- skip_gain: float32 [64], P('tp'), may hold values from 0.1 to 0.5
- inner_gain: bfloat16 [4096], P('tp'), may hold values from 0.25 to 1.75
- out_weight: bfloat16 [4096, 4096], P('tp'), may hold values from -0.09375 to 0.09375
- initial_state: float32 [64, 64, 128], P('tp'), may hold values from -0.3 to 0.3
Outputs:
- new_hidden: bfloat16 [8192, 4096], P('seq', 'tp')
All inputs are finite; a program needn't handle non-finite values.
Results may differ from a plain program's by a relative error of at most 0.009.
Values may be sent and summed in bfloat16 or wider, within the bound.
A program may use at most 128 MiB of HBM per device.

v0:
```python
import jax
import jax.numpy as jnp
from jax import lax
from jax.sharding import PartitionSpec as P

SPAN = 128


EPSILON = 1e-05
PRECISE = lax.Precision.HIGHEST


def from_behind(block, axis, distance):
    devices = range(lax.axis_size(axis))
    route = [(i - distance, i) for i in devices if i - distance in devices]
    return lax.ppermute(block, axis, route)


def causal_filter(padded, kernel, length):
    summed = kernel[0].astype(jnp.float32) * padded[0:length].astype(jnp.float32)
    for offset in range(1, kernel.shape[0]):
        summed = summed + kernel[offset].astype(jnp.float32) * padded[
            offset : offset + length
        ].astype(jnp.float32)
    return jax.nn.silu(summed).astype(jnp.bfloat16)


def block_step(carried, inputs):
    memory, log_total = carried
    values, in_map, out_map, step_size, log_decay = inputs
    head_count = values.shape[1]
    group_count = in_map.shape[1]
    ratio_heads = head_count // group_count
    length = values.shape[0]
    row_pos = lax.broadcasted_iota(jnp.int32, (length, length), 0)
    col_pos = lax.broadcasted_iota(jnp.int32, (length, length), 1)
    causal = row_pos >= col_pos
    cumulative = jnp.cumsum(log_decay, axis=0)
    across = cumulative.T
    spread = across[:, :, None] - across[:, None, :]
    weights = jnp.where(causal[None], jnp.exp(jnp.where(causal[None], spread, 0.0)), 0.0)
    group_scores = jnp.einsum("tgn,sgn->gts", out_map, in_map, preferred_element_type=jnp.float32)
    scores = (
        weights.reshape(group_count, ratio_heads, length, length) * group_scores[:, None]
    ).reshape(head_count, length, length)
    scaled = values * step_size[:, :, None]
    within = jnp.einsum("hts,shp->thp", scores, scaled, precision=PRECISE)
    in_heads = jnp.repeat(in_map.astype(jnp.float32), ratio_heads, axis=1)
    out_heads = jnp.repeat(out_map.astype(jnp.float32), ratio_heads, axis=1)
    from_memory = jnp.einsum(
        "thn,hpn->thp", out_heads * jnp.exp(cumulative)[:, :, None], memory, precision=PRECISE
    )
    final_log = cumulative[-1]
    remaining = jnp.exp(final_log[None, :] - cumulative)
    update = jnp.einsum("shp,shn->hpn", scaled * remaining[:, :, None], in_heads, precision=PRECISE)
    new_memory = jnp.exp(final_log)[:, None, None] * memory + update
    return (
        (new_memory, log_total + final_log),
        (within + from_memory, cumulative + log_total[None, :]),
    )


def run_blocks(values, in_map, out_map, step_size, log_decay, memory):
    blocks = values.shape[0] // SPAN

    def in_blocks(tensor):
        return tensor.reshape((blocks, SPAN) + tensor.shape[1:])

    start_total = jnp.zeros((values.shape[1],), jnp.float32)
    finals, traced = lax.scan(
        block_step,
        (memory, start_total),
        (
            in_blocks(values),
            in_blocks(in_map),
            in_blocks(out_map),
            in_blocks(step_size),
            in_blocks(log_decay),
        ),
    )
    outputs = traced[0].reshape(values.shape)
    cumulative = traced[1].reshape(step_size.shape)
    return (finals[0], finals[1], outputs, cumulative)


def on_device(
    hidden,
    norm_gain,
    gate_x_weight,
    state_weight,
    step_weight,
    conv_inner,
    conv_state,
    step_bias,
    decay_log,
    skip_gain,
    inner_gain,
    out_weight,
    initial_state,
):
    gathered = lax.all_gather(hidden, "tp", axis=1, tiled=True)
    row_count = gathered.shape[0]
    model_width = gathered.shape[1]
    inner_local = gate_x_weight.shape[2]
    state_local = state_weight.shape[2]
    heads_local = step_weight.shape[1]
    head_width = inner_local // heads_local
    state_size = initial_state.shape[2]
    groups_local = state_local // state_size
    hidden_wide = gathered.astype(jnp.float32)
    moments = jnp.mean(hidden_wide * hidden_wide, axis=-1, keepdims=True)
    normed = (hidden_wide * lax.rsqrt(moments + EPSILON) * norm_gain.astype(jnp.float32)).astype(
        jnp.bfloat16
    )
    gate_and_x = (
        jnp.dot(
            normed,
            gate_x_weight.reshape(model_width, 2 * inner_local),
            preferred_element_type=jnp.float32,
        )
        .astype(jnp.bfloat16)
        .reshape(row_count, 2, inner_local)
    )
    state_raw = jnp.dot(
        normed,
        state_weight.reshape(model_width, 2 * state_local),
        preferred_element_type=jnp.float32,
    ).astype(jnp.bfloat16)
    step_raw = jnp.dot(normed, step_weight, preferred_element_type=jnp.float32).astype(jnp.bfloat16)
    inner_raw = gate_and_x[:, 1]
    rim_rows = conv_inner.shape[0] - 1
    tail_rows = jnp.concatenate(
        [inner_raw[row_count - rim_rows :], state_raw[row_count - rim_rows :]], axis=1
    )
    arrived_rim = from_behind(tail_rows, "seq", 1)
    inner_pad = jnp.concatenate([arrived_rim[:, :inner_local], inner_raw], axis=0)
    state_pad = jnp.concatenate([arrived_rim[:, inner_local:], state_raw], axis=0).reshape(
        row_count + rim_rows, 2, state_local
    )
    inner_conv = causal_filter(inner_pad, conv_inner, row_count)
    state_conv = causal_filter(state_pad, conv_state, row_count)
    step_size = jax.nn.softplus(step_raw.astype(jnp.float32) + step_bias[None, :])
    log_decay = -step_size * jnp.exp(decay_log)[None, :]
    values = inner_conv.astype(jnp.float32).reshape(row_count, heads_local, head_width)
    in_map = state_conv[:, 0].reshape(row_count, groups_local, state_size)
    out_map = state_conv[:, 1].reshape(row_count, groups_local, state_size)
    memory_zero = jnp.zeros_like(initial_state)
    local_memory, local_total, outputs, cumulative = run_blocks(
        values, in_map, out_map, step_size, log_decay, memory_zero
    )
    decay_all = jnp.exp(local_total)
    first_mask = (lax.axis_index("seq") == 0).astype(jnp.float32)

    def relay_turn(turn_index, incoming):
        leaving = decay_all[:, None, None] * incoming + local_memory
        arrived_state = from_behind(leaving, "seq", 1)
        return arrived_state + first_mask * initial_state

    entering = lax.fori_loop(0, lax.axis_size("seq") - 1, relay_turn, first_mask * initial_state)
    out_heads = jnp.repeat(out_map.astype(jnp.float32), heads_local // groups_local, axis=1)
    correction = jnp.einsum(
        "thn,hpn->thp", out_heads * jnp.exp(cumulative)[:, :, None], entering, precision=PRECISE
    )
    mixer_out = outputs + correction + skip_gain[None, :, None] * values
    gated_out = mixer_out.reshape(row_count, inner_local) * jax.nn.silu(
        gate_and_x[:, 0].astype(jnp.float32)
    )
    grouped = gated_out.reshape(row_count, groups_local, inner_local // groups_local)
    scale_rows = lax.rsqrt(jnp.mean(grouped * grouped, axis=-1, keepdims=True) + EPSILON)
    mixed_rows = (
        (grouped * scale_rows).reshape(row_count, inner_local) * inner_gain.astype(jnp.float32)
    ).astype(jnp.bfloat16)
    partial_terms = jnp.dot(mixed_rows, out_weight, preferred_element_type=jnp.float32)
    projected = lax.psum_scatter(partial_terms, "tp", scatter_dimension=1, tiled=True)
    return (projected + hidden.astype(jnp.float32)).astype(jnp.bfloat16)


def solution(mesh):
    return jax.shard_map(
        on_device,
        mesh=mesh,
        in_specs=(
            P("seq", "tp"),
            P(),
            P(None, None, "tp"),
            P(None, None, "tp"),
            P(None, "tp"),
            P(None, "tp"),
            P(None, None, "tp"),
            P("tp"),
            P("tp"),
            P("tp"),
            P("tp"),
            P("tp", None),
            P("tp", None, None),
        ),
        out_specs=P("seq", "tp"),
        check_vma=False,
    )
```

profile of v0, /device:TPU:1, one launch (start us, length us, event | category | flops | bytes accessed | tf_op | source)
XLA Modules:
  0.0 380.8 jit_solution(123641750250642772)
XLA Ops:
  8.1 9.4 %copy.94 = bf16[512,8,2,512]{3,1,2,0:T(8,128)(2,1)} copy(bf16[512,8,2,512]{3,2,1,0:T(2,128)(2,1)} %bitcast.162) | data formatting | bytes 16777216
  18.1 26.9 %all-gather.2.cloned.1.call-done = bf16[512,4096]{1,0:T(8,128)(2,1)} async-done(((bf16[512,512]{1,0:T(8,128)(2,1)}), bf16[512,4096]{1,0:T(8,128)(2,1)}) %all-gather.2.cloned.1.call-update) | async-done | bytes 4194320 | tf_op jit(solution)/shard_map/all_gather | solution.py:101
  45.0 3.2 fusion.35
  48.5 7.2 %convolution_convert_fusion = bf16[512,1024]{1,0:T(8,128)(2,1)S(1)} fusion(bf16[4096,1024]{1,0:T(8,128)(2,1)} %bitcast.163, bf16[512,4096]{1,0:T(8,128)(2,1)S(1)} %copy-done.3, f32[4096]{0:T(1024)S(1)} %convert_element_type.120, f32[512]{0:T(512)S(1)} %add_rsqrt_fusion.1), kind=kOutput, calls=%fused_computation.60 | convolution fusion | flops 4303880192 | bytes 13649920 | tf_op jit(solution)/shard_map/dot_general | solution.py:116
  56.6 4.3 %fusion.52 = bf16[512,256]{1,0:T(8,128)(2,1)S(1)} fusion(bf16[512,8,2,128]{3,2,1,0:T(2,128)(2,1)} %bitcast.179, bf16[512,4096]{1,0:T(8,128)(2,1)} %all-gather.2.cloned.1.call-done, f32[4096]{0:T(1024)S(1)} %convert_element_type.120, f32[512]{0:T(512)S(1)} %add_rsqrt_fusion.1), kind=kOutput, calls=%fused_computation.66 | convolution fusion | flops 1082261504 | bytes 6572032 | tf_op jit(solution)/shard_map/dot_general | solution.py:124
  61.0 3.2 collective-permute-start.1
  74.8 61.1 %while.28 = (s32[]{:T(128)}, f32[8,64,128]{2,1,0:T(8,128)S(1)}, f32[8]{0:T(128)S(1)}, f32[4,128,8,64]{1,0,3,2:T(4,128)}, f32[4,128,8]{2,1,0:T(8,128)}, /*index=5...) while((s32[]{:T(128)}, f32[8,64,128]{2,1,0:T(8,128)S(1)}, ...), condition=%wide.region_3.4_spmd.clone, body=%wide.region_1.3_spmd.clone.sunk | while | flops 307545088 | bytes 3345373 | solution.py:70
  76.1 2.1 convolution_bitcast_fusion.3
  80.3 7.5 %dynamic_update_slice.14 = f32[4,128,8,64]{1,0,3,2:T(4,128)} dynamic-update-slice(f32[4,128,8,64]{1,0,3,2:T(4,128)} %get-tuple-element.354, f32[1,128,8,64]{1,0,3,2:T(1,128)S(1)} %bitcast.161, s32[]{:T(128)} %get-tuple-element.351, s32[]{:T(128)} %constant.34.clone.1..sunk, s32[]{:T(128)} %constant.34.clone.1..sunk, s32[]{:T(128)} %constant.34.clone.1..sunk) | dynamic-update-slice | bytes 524292 | tf_op jit(solution)/shard_map/while/body/jit(dynamic_update_index_in_dim)/dynamic_update_slice | solution.py:70
  95.6 7.5 %dynamic_update_slice.14 = f32[4,128,8,64]{1,0,3,2:T(4,128)} dynamic-update-slice(f32[4,128,8,64]{1,0,3,2:T(4,128)} %get-tuple-element.354, f32[1,128,8,64]{1,0,3,2:T(1,128)S(1)} %bitcast.161, s32[]{:T(128)} %get-tuple-element.351, s32[]{:T(128)} %constant.34.clone.1..sunk, s32[]{:T(128)} %constant.34.clone.1..sunk, s32[]{:T(128)} %constant.34.clone.1..sunk) | dynamic-update-slice | bytes 524292 | tf_op jit(solution)/shard_map/while/body/jit(dynamic_update_index_in_dim)/dynamic_update_slice | solution.py:70
  110.9 7.5 %dynamic_update_slice.14 = f32[4,128,8,64]{1,0,3,2:T(4,128)} dynamic-update-slice(f32[4,128,8,64]{1,0,3,2:T(4,128)} %get-tuple-element.354, f32[1,128,8,64]{1,0,3,2:T(1,128)S(1)} %bitcast.161, s32[]{:T(128)} %get-tuple-element.351, s32[]{:T(128)} %constant.34.clone.1..sunk, s32[]{:T(128)} %constant.34.clone.1..sunk, s32[]{:T(128)} %constant.34.clone.1..sunk) | dynamic-update-slice | bytes 524292 | tf_op jit(solution)/shard_map/while/body/jit(dynamic_update_index_in_dim)/dynamic_update_slice | solution.py:70
  126.1 7.5 %dynamic_update_slice.14 = f32[4,128,8,64]{1,0,3,2:T(4,128)} dynamic-update-slice(f32[4,128,8,64]{1,0,3,2:T(4,128)} %get-tuple-element.354, f32[1,128,8,64]{1,0,3,2:T(1,128)S(1)} %bitcast.161, s32[]{:T(128)} %get-tuple-element.351, s32[]{:T(128)} %constant.34.clone.1..sunk, s32[]{:T(128)} %constant.34.clone.1..sunk, s32[]{:T(128)} %constant.34.clone.1..sunk) | dynamic-update-slice | bytes 524292 | tf_op jit(solution)/shard_map/while/body/jit(dynamic_update_index_in_dim)/dynamic_update_slice | solution.py:70
  135.9 2.6 reshape.192
  139.6 139.5 %while.27 = (s32[]{:T(128)}, f32[8,64,128]{2,1,0:T(8,128)S(1)}, f32[8]{0:T(128)S(1)}, f32[8,64,128]{2,1,0:T(8,128)S(1)}, f32[]{:T(128)}, /*index=5*/f32[8,64,128]{2,1,0:T(8,128)S(1)}, s32[]{:T(128)}) while((s32[]{:T(128)}, f32[8,64,128]{2,1,0:T(8,128)S(1)}, f32[8]{0:T(128)S(1)}, f32[8,64,128]{2,1,0:T(8,128)S(1)}, f32[]{:T(128)}, ...), condition=%wide.region_5.6_spmd, body=%wide.region_4.5_spmd.sunk | while | flops 262146 | bytes 2621593 | solution.py:159
  139.7 3.3 collective-permute-start
  143.0 5.1 %collective-permute-done = f32[8,64,128]{2,1,0:T(8,128)S(1)} collective-permute-done((f32[8,64,128]{2,1,0:T(8,128)S(1)}, f32[8,64,128]{2,1,0:T(8,128)S(1)}, u32[]{:S(2)}, u32[]{:S(2)}) %collective-permute-start) | collective-permute-done | bytes 262176 | tf_op jit(solution)/shard_map/while/body/eval_jaxpr/ppermute | solution.py:16
  148.3 4.1 %collective-permute-start = (f32[8,64,128]{2,1,0:T(8,128)S(1)}, f32[8,64,128]{2,1,0:T(8,128)S(1)}, u32[]{:S(2)}, u32[]{:S(2)}) collective-permute-start(f32[8,64,128]{2,1,0:T(8,128)S(1)} %multiply_add_fusion.4), channel_id=1, source_target_pairs={{0,8},{8,16},{16,24},{24,32},{32,40},{40,48},{48,56},{56,64},{64,7... | collective-permute-start | bytes 786440 | tf_op jit(solution)/shard_map/while/body/eval_jaxpr/ppermute | solution.py:16
  152.4 4.2 %collective-permute-done = f32[8,64,128]{2,1,0:T(8,128)S(1)} collective-permute-done((f32[8,64,128]{2,1,0:T(8,128)S(1)}, f32[8,64,128]{2,1,0:T(8,128)S(1)}, u32[]{:S(2)}, u32[]{:S(2)}) %collective-permute-start) | collective-permute-done | bytes 262176 | tf_op jit(solution)/shard_map/while/body/eval_jaxpr/ppermute | solution.py:16
  156.7 4.1 %collective-permute-start = (f32[8,64,128]{2,1,0:T(8,128)S(1)}, f32[8,64,128]{2,1,0:T(8,128)S(1)}, u32[]{:S(2)}, u32[]{:S(2)}) collective-permute-start(f32[8,64,128]{2,1,0:T(8,128)S(1)} %multiply_add_fusion.4), channel_id=1, source_target_pairs={{0,8},{8,16},{16,24},{24,32},{32,40},{40,48},{48,56},{56,64},{64,7... | collective-permute-start | bytes 786440 | tf_op jit(solution)/shard_map/while/body/eval_jaxpr/ppermute | solution.py:16
  160.8 3.3 collective-permute-done
  164.3 3.8 %collective-permute-start = (f32[8,64,128]{2,1,0:T(8,128)S(1)}, f32[8,64,128]{2,1,0:T(8,128)S(1)}, u32[]{:S(2)}, u32[]{:S(2)}) collective-permute-start(f32[8,64,128]{2,1,0:T(8,128)S(1)} %multiply_add_fusion.4), channel_id=1, source_target_pairs={{0,8},{8,16},{16,24},{24,32},{32,40},{40,48},{48,56},{56,64},{64,7... | collective-permute-start | bytes 786440 | tf_op jit(solution)/shard_map/while/body/eval_jaxpr/ppermute | solution.py:16
  168.1 3.3 collective-permute-done
  171.5 3.8 %collective-permute-start = (f32[8,64,128]{2,1,0:T(8,128)S(1)}, f32[8,64,128]{2,1,0:T(8,128)S(1)}, u32[]{:S(2)}, u32[]{:S(2)}) collective-permute-start(f32[8,64,128]{2,1,0:T(8,128)S(1)} %multiply_add_fusion.4), channel_id=1, source_target_pairs={{0,8},{8,16},{16,24},{24,32},{32,40},{40,48},{48,56},{56,64},{64,7... | collective-permute-start | bytes 786440 | tf_op jit(solution)/shard_map/while/body/eval_jaxpr/ppermute | solution.py:16
  175.4 3.3 collective-permute-done
  178.8 4.1 %collective-permute-start = (f32[8,64,128]{2,1,0:T(8,128)S(1)}, f32[8,64,128]{2,1,0:T(8,128)S(1)}, u32[]{:S(2)}, u32[]{:S(2)}) collective-permute-start(f32[8,64,128]{2,1,0:T(8,128)S(1)} %multiply_add_fusion.4), channel_id=1, source_target_pairs={{0,8},{8,16},{16,24},{24,32},{32,40},{40,48},{48,56},{56,64},{64,7... | collective-permute-start | bytes 786440 | tf_op jit(solution)/shard_map/while/body/eval_jaxpr/ppermute | solution.py:16
  182.9 3.7 collective-permute-done
  186.7 5.5 %collective-permute-start = (f32[8,64,128]{2,1,0:T(8,128)S(1)}, f32[8,64,128]{2,1,0:T(8,128)S(1)}, u32[]{:S(2)}, u32[]{:S(2)}) collective-permute-start(f32[8,64,128]{2,1,0:T(8,128)S(1)} %multiply_add_fusion.4), channel_id=1, source_target_pairs={{0,8},{8,16},{16,24},{24,32},{32,40},{40,48},{48,56},{56,64},{64,7... | collective-permute-start | bytes 786440 | tf_op jit(solution)/shard_map/while/body/eval_jaxpr/ppermute | solution.py:16
  192.2 3.3 collective-permute-done
  195.7 6.2 %collective-permute-start = (f32[8,64,128]{2,1,0:T(8,128)S(1)}, f32[8,64,128]{2,1,0:T(8,128)S(1)}, u32[]{:S(2)}, u32[]{:S(2)}) collective-permute-start(f32[8,64,128]{2,1,0:T(8,128)S(1)} %multiply_add_fusion.4), channel_id=1, source_target_pairs={{0,8},{8,16},{16,24},{24,32},{32,40},{40,48},{48,56},{56,64},{64,7... | collective-permute-start | bytes 786440 | tf_op jit(solution)/shard_map/while/body/eval_jaxpr/ppermute | solution.py:16
  201.9 4.3 %collective-permute-done = f32[8,64,128]{2,1,0:T(8,128)S(1)} collective-permute-done((f32[8,64,128]{2,1,0:T(8,128)S(1)}, f32[8,64,128]{2,1,0:T(8,128)S(1)}, u32[]{:S(2)}, u32[]{:S(2)}) %collective-permute-start) | collective-permute-done | bytes 262176 | tf_op jit(solution)/shard_map/while/body/eval_jaxpr/ppermute | solution.py:16
  206.3 6.5 %collective-permute-start = (f32[8,64,128]{2,1,0:T(8,128)S(1)}, f32[8,64,128]{2,1,0:T(8,128)S(1)}, u32[]{:S(2)}, u32[]{:S(2)}) collective-permute-start(f32[8,64,128]{2,1,0:T(8,128)S(1)} %multiply_add_fusion.4), channel_id=1, source_target_pairs={{0,8},{8,16},{16,24},{24,32},{32,40},{40,48},{48,56},{56,64},{64,7... | collective-permute-start | bytes 786440 | tf_op jit(solution)/shard_map/while/body/eval_jaxpr/ppermute | solution.py:16
  212.9 5.4 %collective-permute-done = f32[8,64,128]{2,1,0:T(8,128)S(1)} collective-permute-done((f32[8,64,128]{2,1,0:T(8,128)S(1)}, f32[8,64,128]{2,1,0:T(8,128)S(1)}, u32[]{:S(2)}, u32[]{:S(2)}) %collective-permute-start) | collective-permute-done | bytes 262176 | tf_op jit(solution)/shard_map/while/body/eval_jaxpr/ppermute | solution.py:16
  218.4 6.9 %collective-permute-start = (f32[8,64,128]{2,1,0:T(8,128)S(1)}, f32[8,64,128]{2,1,0:T(8,128)S(1)}, u32[]{:S(2)}, u32[]{:S(2)}) collective-permute-start(f32[8,64,128]{2,1,0:T(8,128)S(1)} %multiply_add_fusion.4), channel_id=1, source_target_pairs={{0,8},{8,16},{16,24},{24,32},{32,40},{40,48},{48,56},{56,64},{64,7... | collective-permute-start | bytes 786440 | tf_op jit(solution)/shard_map/while/body/eval_jaxpr/ppermute | solution.py:16
  225.3 5.5 %collective-permute-done = f32[8,64,128]{2,1,0:T(8,128)S(1)} collective-permute-done((f32[8,64,128]{2,1,0:T(8,128)S(1)}, f32[8,64,128]{2,1,0:T(8,128)S(1)}, u32[]{:S(2)}, u32[]{:S(2)}) %collective-permute-start) | collective-permute-done | bytes 262176 | tf_op jit(solution)/shard_map/while/body/eval_jaxpr/ppermute | solution.py:16
  231.0 6.3 %collective-permute-start = (f32[8,64,128]{2,1,0:T(8,128)S(1)}, f32[8,64,128]{2,1,0:T(8,128)S(1)}, u32[]{:S(2)}, u32[]{:S(2)}) collective-permute-start(f32[8,64,128]{2,1,0:T(8,128)S(1)} %multiply_add_fusion.4), channel_id=1, source_target_pairs={{0,8},{8,16},{16,24},{24,32},{32,40},{40,48},{48,56},{56,64},{64,7... | collective-permute-start | bytes 786440 | tf_op jit(solution)/shard_map/while/body/eval_jaxpr/ppermute | solution.py:16
  237.3 4.4 %collective-permute-done = f32[8,64,128]{2,1,0:T(8,128)S(1)} collective-permute-done((f32[8,64,128]{2,1,0:T(8,128)S(1)}, f32[8,64,128]{2,1,0:T(8,128)S(1)}, u32[]{:S(2)}, u32[]{:S(2)}) %collective-permute-start) | collective-permute-done | bytes 262176 | tf_op jit(solution)/shard_map/while/body/eval_jaxpr/ppermute | solution.py:16
  241.8 4.9 %collective-permute-start = (f32[8,64,128]{2,1,0:T(8,128)S(1)}, f32[8,64,128]{2,1,0:T(8,128)S(1)}, u32[]{:S(2)}, u32[]{:S(2)}) collective-permute-start(f32[8,64,128]{2,1,0:T(8,128)S(1)} %multiply_add_fusion.4), channel_id=1, source_target_pairs={{0,8},{8,16},{16,24},{24,32},{32,40},{40,48},{48,56},{56,64},{64,7... | collective-permute-start | bytes 786440 | tf_op jit(solution)/shard_map/while/body/eval_jaxpr/ppermute | solution.py:16
  246.8 3.3 collective-permute-done
  250.2 6.2 %collective-permute-start = (f32[8,64,128]{2,1,0:T(8,128)S(1)}, f32[8,64,128]{2,1,0:T(8,128)S(1)}, u32[]{:S(2)}, u32[]{:S(2)}) collective-permute-start(f32[8,64,128]{2,1,0:T(8,128)S(1)} %multiply_add_fusion.4), channel_id=1, source_target_pairs={{0,8},{8,16},{16,24},{24,32},{32,40},{40,48},{48,56},{56,64},{64,7... | collective-permute-start | bytes 786440 | tf_op jit(solution)/shard_map/while/body/eval_jaxpr/ppermute | solution.py:16
  256.4 3.3 collective-permute-done
  259.9 6.2 %collective-permute-start = (f32[8,64,128]{2,1,0:T(8,128)S(1)}, f32[8,64,128]{2,1,0:T(8,128)S(1)}, u32[]{:S(2)}, u32[]{:S(2)}) collective-permute-start(f32[8,64,128]{2,1,0:T(8,128)S(1)} %multiply_add_fusion.4), channel_id=1, source_target_pairs={{0,8},{8,16},{16,24},{24,32},{32,40},{40,48},{48,56},{56,64},{64,7... | collective-permute-start | bytes 786440 | tf_op jit(solution)/shard_map/while/body/eval_jaxpr/ppermute | solution.py:16
  266.1 3.3 collective-permute-done
  269.5 6.2 %collective-permute-start = (f32[8,64,128]{2,1,0:T(8,128)S(1)}, f32[8,64,128]{2,1,0:T(8,128)S(1)}, u32[]{:S(2)}, u32[]{:S(2)}) collective-permute-start(f32[8,64,128]{2,1,0:T(8,128)S(1)} %multiply_add_fusion.4), channel_id=1, source_target_pairs={{0,8},{8,16},{16,24},{24,32},{32,40},{40,48},{48,56},{56,64},{64,7... | collective-permute-start | bytes 786440 | tf_op jit(solution)/shard_map/while/body/eval_jaxpr/ppermute | solution.py:16
  275.8 3.3 collective-permute-done
  279.1 4.7 %fusion.49 = f32[512,8,64]{0,2,1:T(8,128)} fusion(f32[512,8,64]{0,2,1:T(8,128)} %reshape.192, f32[8,64,128]{2,1,0:T(8,128)S(1)} %get-tuple-element.95, f32[512,8,64]{0,2,1:T(8,128)S(1)} %bitcast.167, f32[512,8]{0,1:T(8,128)S(1)} %copy.77, f32[512,128]{1,0:T(8,128)S(1)} %copy-done.7, f32[8]{0:T(128)S(1)} %copy-done.14), kind=kOutput, calls=%fused_computation.63 | convolution fusion | flops 403963904 | bytes 3686432 | tf_op jit(solution)/shard_map/thn,hpn->thp/dot_general | solution.py:161
  285.8 8.0 %fusion.66 = f32[512,4096]{1,0:T(8,128)} fusion(bf16[512,4096]{1,0:T(8,128)(2,1)} %param.28, f32[512]{0:T(512)S(1)} %convert_element_type.145, f32[512]{0:T(512)S(1)} %add_rsqrt_fusion, f32[512,1,512]{2,0,1:T(8,128)S(1)} %copy.80, bf16[512,1,512]{2,0,1:T(8,128)(2,1)S(1)} %copy.87), kind=kOutput, calls=%fused_computation.85 | convolution fusion | flops 2149842944 | bytes 14159872 | tf_op jit(solution)/shard_map/dot_general | solution.py:173
  293.8 78.0 %reduce-scatter.2.cloned.1.call-done = f32[512,512]{1,0:T(8,128)} async-done(((f32[512,4096]{1,0:T(8,128)}), f32[512,512]{1,0:T(8,128)}) %reduce-scatter.2.cloned.1.call-update) | async-done | bytes 1048592 | tf_op jit(solution)/shard_map/reduce_scatter | solution.py:174
  371.8 2.2 add_convert_fusion
  (172 shorter events, 47.2 us)
Async XLA Ops:
  6.5 57.7 %copy-start = (bf16[4096,8]{0,1:T(8,128)(2,1)S(1)}, bf16[4096,8]{0,1:T(8,128)(2,1)}, u32[]{:S(2)}) copy-start(bf16[4096,8]{0,1:T(8,128)(2,1)} %param.21) | copy-start | bytes 196612
  6.5 38.5 %all-gather.2.cloned.1.call-start = ((), (), s32[]{:S(2)}) async-start(), calls=%async_computation.1 | async-start | bytes 4718592 | tf_op jit(solution)/shard_map/all_gather | solution.py:101
  7.3 364.6 %reduce-scatter.2.cloned.1.call-start = ((), (), s32[]{:S(2)}) async-start(), calls=%async_computation.2 | async-start | bytes 9437184 | tf_op jit(solution)/shard_map/reduce_scatter | solution.py:174
  8.0 9.4 %copy-start.15 = (f32[8]{0:T(128)S(1)}, f32[8]{0:T(128)}, u32[]{:S(2)}) copy-start(f32[8]{0:T(128)} %param.25) | copy-start | bytes 100
  8.1 10.0 %copy-start.12 = (bf16[512]{0:T(512)(128)(2,1)S(1)}, bf16[512]{0:T(512)(128)(2,1)}, u32[]{:S(2)}) copy-start(bf16[512]{0:T(512)(128)(2,1)} %param.27) | copy-start | bytes 3076
  8.1 10.0 %copy-start.10 = (bf16[4,2,128]{2,1,0:T(2,128)(2,1)S(1)}, bf16[4,2,128]{2,1,0:T(2,128)(2,1)}, u32[]{:S(2)}) copy-start(bf16[4,2,128]{2,1,0:T(2,128)(2,1)} %param.23) | copy-start | bytes 6148
  8.1 10.0 %copy-start.9 = (bf16[4,512]{1,0:T(4,128)(2,1)S(1)}, bf16[4,512]{1,0:T(4,128)(2,1)}, u32[]{:S(2)}) copy-start(bf16[4,512]{1,0:T(4,128)(2,1)} %param.22) | copy-start | bytes 12292
  8.1 10.0 %copy-start.1 = (f32[8,64,128]{2,1,0:T(8,128)S(1)}, f32[8,64,128]{2,1,0:T(8,128)}, u32[]{:S(2)}) copy-start(f32[8,64,128]{2,1,0:T(8,128)} %param.29) | copy-start | bytes 786436
  45.0 3.4 copy-start.3
  48.3 8.3 %copy-start.11 = (f32[512]{0:T(512)}, f32[512]{0:T(512)S(1)}, u32[]{:S(2)}) copy-start(f32[512]{0:T(512)S(1)} %add_rsqrt_fusion.1) | copy-start | bytes 6148
  56.5 7.7 %copy-start.4 = (bf16[512,4096]{1,0:T(8,128)(2,1)S(1)}, bf16[512,4096]{1,0:T(8,128)(2,1)}, u32[]{:S(2)}) copy-start(bf16[512,4096]{1,0:T(8,128)(2,1)} %all-gather.2.cloned.1.call-done) | copy-start | bytes 12582916
  56.5 7.7 %copy-start.16 = (f32[8]{0:T(128)S(1)}, f32[8]{0:T(128)}, u32[]{:S(2)}) copy-start(f32[8]{0:T(128)} %param.24) | copy-start | bytes 100
  60.9 5.4 %copy-start.8 = (bf16[512,256]{1,0:T(8,128)(2,1)}, bf16[512,256]{1,0:T(8,128)(2,1)S(1)}, u32[]{:S(2)}) copy-start(bf16[512,256]{1,0:T(8,128)(2,1)S(1)} %fusion.52) | copy-start | bytes 786436
  60.9 5.3 %copy-start.13 = (f32[8]{0:T(128)S(1)}, f32[8]{0:T(128)}, u32[]{:S(2)}) copy-start(f32[8]{0:T(128)} %exp.60) | copy-start | bytes 100
  61.0 5.8 %collective-permute-start.1 = (bf16[3,768]{1,0:T(4,128)(2,1)S(1)}, bf16[3,768]{1,0:T(4,128)(2,1)S(1)}, u32[]{:S(2)}, u32[]{:S(2)}) collective-permute-start(bf16[3,768]{1,0:T(4,128)(2,1)S(1)} %pad_maximum_fusion.2), channel_id=1, source_target_pairs={{0,8},{8,16},{16,24},{24,32},{32,40},{40,48},{48,56},{56,64},{64,7... | collective-permute-start | bytes 13832 | tf_op jit(solution)/shard_map/ppermute | solution.py:16
  70.5 2.6 copy-start.2
  139.5 139.6 %copy-start.5 = (f32[512,512]{0,1:T(8,128)S(1)}, f32[512,512]{0,1:T(8,128)}, u32[]{:S(2)}) copy-start(f32[512,512]{0,1:T(8,128)} %copy.78) | copy-start | bytes 3145732
  139.5 139.6 %copy-start.7 = (f32[512,128]{1,0:T(8,128)S(1)}, f32[512,128]{1,0:T(8,128)}, u32[]{:S(2)}) copy-start(f32[512,128]{1,0:T(8,128)} %get-tuple-element.214) | copy-start | bytes 786436
  139.5 139.6 %copy-start.14 = (f32[8]{0:T(128)S(1)}, f32[8]{0:T(128)}, u32[]{:S(2)}) copy-start(f32[8]{0:T(128)} %param.26) | copy-start | bytes 100
  139.7 8.4 %collective-permute-start = (f32[8,64,128]{2,1,0:T(8,128)S(1)}, f32[8,64,128]{2,1,0:T(8,128)S(1)}, u32[]{:S(2)}, u32[]{:S(2)}) collective-permute-start(f32[8,64,128]{2,1,0:T(8,128)S(1)} %multiply_add_fusion.4), channel_id=1, source_target_pairs={{0,8},{8,16},{16,24},{24,32},{32,40},{40,48},{48,56},{56,64},{64,7... | collective-permute-start | bytes 786440 | tf_op jit(solution)/shard_map/while/body/eval_jaxpr/ppermute | solution.py:16
  148.3 8.3 %collective-permute-start = (f32[8,64,128]{2,1,0:T(8,128)S(1)}, f32[8,64,128]{2,1,0:T(8,128)S(1)}, u32[]{:S(2)}, u32[]{:S(2)}) collective-permute-start(f32[8,64,128]{2,1,0:T(8,128)S(1)} %multiply_add_fusion.4), channel_id=1, source_target_pairs={{0,8},{8,16},{16,24},{24,32},{32,40},{40,48},{48,56},{56,64},{64,7... | collective-permute-start | bytes 786440 | tf_op jit(solution)/shard_map/while/body/eval_jaxpr/ppermute | solution.py:16
  156.7 7.4 %collective-permute-start = (f32[8,64,128]{2,1,0:T(8,128)S(1)}, f32[8,64,128]{2,1,0:T(8,128)S(1)}, u32[]{:S(2)}, u32[]{:S(2)}) collective-permute-start(f32[8,64,128]{2,1,0:T(8,128)S(1)} %multiply_add_fusion.4), channel_id=1, source_target_pairs={{0,8},{8,16},{16,24},{24,32},{32,40},{40,48},{48,56},{56,64},{64,7... | collective-permute-start | bytes 786440 | tf_op jit(solution)/shard_map/while/body/eval_jaxpr/ppermute | solution.py:16
  164.3 7.1 %collective-permute-start = (f32[8,64,128]{2,1,0:T(8,128)S(1)}, f32[8,64,128]{2,1,0:T(8,128)S(1)}, u32[]{:S(2)}, u32[]{:S(2)}) collective-permute-start(f32[8,64,128]{2,1,0:T(8,128)S(1)} %multiply_add_fusion.4), channel_id=1, source_target_pairs={{0,8},{8,16},{16,24},{24,32},{32,40},{40,48},{48,56},{56,64},{64,7... | collective-permute-start | bytes 786440 | tf_op jit(solution)/shard_map/while/body/eval_jaxpr/ppermute | solution.py:16
  171.5 7.1 %collective-permute-start = (f32[8,64,128]{2,1,0:T(8,128)S(1)}, f32[8,64,128]{2,1,0:T(8,128)S(1)}, u32[]{:S(2)}, u32[]{:S(2)}) collective-permute-start(f32[8,64,128]{2,1,0:T(8,128)S(1)} %multiply_add_fusion.4), channel_id=1, source_target_pairs={{0,8},{8,16},{16,24},{24,32},{32,40},{40,48},{48,56},{56,64},{64,7... | collective-permute-start | bytes 786440 | tf_op jit(solution)/shard_map/while/body/eval_jaxpr/ppermute | solution.py:16
  178.8 7.8 %collective-permute-start = (f32[8,64,128]{2,1,0:T(8,128)S(1)}, f32[8,64,128]{2,1,0:T(8,128)S(1)}, u32[]{:S(2)}, u32[]{:S(2)}) collective-permute-start(f32[8,64,128]{2,1,0:T(8,128)S(1)} %multiply_add_fusion.4), channel_id=1, source_target_pairs={{0,8},{8,16},{16,24},{24,32},{32,40},{40,48},{48,56},{56,64},{64,7... | collective-permute-start | bytes 786440 | tf_op jit(solution)/shard_map/while/body/eval_jaxpr/ppermute | solution.py:16
  186.7 8.8 %collective-permute-start = (f32[8,64,128]{2,1,0:T(8,128)S(1)}, f32[8,64,128]{2,1,0:T(8,128)S(1)}, u32[]{:S(2)}, u32[]{:S(2)}) collective-permute-start(f32[8,64,128]{2,1,0:T(8,128)S(1)} %multiply_add_fusion.4), channel_id=1, source_target_pairs={{0,8},{8,16},{16,24},{24,32},{32,40},{40,48},{48,56},{56,64},{64,7... | collective-permute-start | bytes 786440 | tf_op jit(solution)/shard_map/while/body/eval_jaxpr/ppermute | solution.py:16
  195.7 10.5 %collective-permute-start = (f32[8,64,128]{2,1,0:T(8,128)S(1)}, f32[8,64,128]{2,1,0:T(8,128)S(1)}, u32[]{:S(2)}, u32[]{:S(2)}) collective-permute-start(f32[8,64,128]{2,1,0:T(8,128)S(1)} %multiply_add_fusion.4), channel_id=1, source_target_pairs={{0,8},{8,16},{16,24},{24,32},{32,40},{40,48},{48,56},{56,64},{64,7... | collective-permute-start | bytes 786440 | tf_op jit(solution)/shard_map/while/body/eval_jaxpr/ppermute | solution.py:16
  206.3 11.9 %collective-permute-start = (f32[8,64,128]{2,1,0:T(8,128)S(1)}, f32[8,64,128]{2,1,0:T(8,128)S(1)}, u32[]{:S(2)}, u32[]{:S(2)}) collective-permute-start(f32[8,64,128]{2,1,0:T(8,128)S(1)} %multiply_add_fusion.4), channel_id=1, source_target_pairs={{0,8},{8,16},{16,24},{24,32},{32,40},{40,48},{48,56},{56,64},{64,7... | collective-permute-start | bytes 786440 | tf_op jit(solution)/shard_map/while/body/eval_jaxpr/ppermute | solution.py:16
  218.4 12.4 %collective-permute-start = (f32[8,64,128]{2,1,0:T(8,128)S(1)}, f32[8,64,128]{2,1,0:T(8,128)S(1)}, u32[]{:S(2)}, u32[]{:S(2)}) collective-permute-start(f32[8,64,128]{2,1,0:T(8,128)S(1)} %multiply_add_fusion.4), channel_id=1, source_target_pairs={{0,8},{8,16},{16,24},{24,32},{32,40},{40,48},{48,56},{56,64},{64,7... | collective-permute-start | bytes 786440 | tf_op jit(solution)/shard_map/while/body/eval_jaxpr/ppermute | solution.py:16
  231.0 10.7 %collective-permute-start = (f32[8,64,128]{2,1,0:T(8,128)S(1)}, f32[8,64,128]{2,1,0:T(8,128)S(1)}, u32[]{:S(2)}, u32[]{:S(2)}) collective-permute-start(f32[8,64,128]{2,1,0:T(8,128)S(1)} %multiply_add_fusion.4), channel_id=1, source_target_pairs={{0,8},{8,16},{16,24},{24,32},{32,40},{40,48},{48,56},{56,64},{64,7... | collective-permute-start | bytes 786440 | tf_op jit(solution)/shard_map/while/body/eval_jaxpr/ppermute | solution.py:16
  241.8 8.2 %collective-permute-start = (f32[8,64,128]{2,1,0:T(8,128)S(1)}, f32[8,64,128]{2,1,0:T(8,128)S(1)}, u32[]{:S(2)}, u32[]{:S(2)}) collective-permute-start(f32[8,64,128]{2,1,0:T(8,128)S(1)} %multiply_add_fusion.4), channel_id=1, source_target_pairs={{0,8},{8,16},{16,24},{24,32},{32,40},{40,48},{48,56},{56,64},{64,7... | collective-permute-start | bytes 786440 | tf_op jit(solution)/shard_map/while/body/eval_jaxpr/ppermute | solution.py:16
  250.2 9.5 %collective-permute-start = (f32[8,64,128]{2,1,0:T(8,128)S(1)}, f32[8,64,128]{2,1,0:T(8,128)S(1)}, u32[]{:S(2)}, u32[]{:S(2)}) collective-permute-start(f32[8,64,128]{2,1,0:T(8,128)S(1)} %multiply_add_fusion.4), channel_id=1, source_target_pairs={{0,8},{8,16},{16,24},{24,32},{32,40},{40,48},{48,56},{56,64},{64,7... | collective-permute-start | bytes 786440 | tf_op jit(solution)/shard_map/while/body/eval_jaxpr/ppermute | solution.py:16
  259.9 9.5 %collective-permute-start = (f32[8,64,128]{2,1,0:T(8,128)S(1)}, f32[8,64,128]{2,1,0:T(8,128)S(1)}, u32[]{:S(2)}, u32[]{:S(2)}) collective-permute-start(f32[8,64,128]{2,1,0:T(8,128)S(1)} %multiply_add_fusion.4), channel_id=1, source_target_pairs={{0,8},{8,16},{16,24},{24,32},{32,40},{40,48},{48,56},{56,64},{64,7... | collective-permute-start | bytes 786440 | tf_op jit(solution)/shard_map/while/body/eval_jaxpr/ppermute | solution.py:16
  269.5 9.5 %collective-permute-start = (f32[8,64,128]{2,1,0:T(8,128)S(1)}, f32[8,64,128]{2,1,0:T(8,128)S(1)}, u32[]{:S(2)}, u32[]{:S(2)}) collective-permute-start(f32[8,64,128]{2,1,0:T(8,128)S(1)} %multiply_add_fusion.4), channel_id=1, source_target_pairs={{0,8},{8,16},{16,24},{24,32},{32,40},{40,48},{48,56},{56,64},{64,7... | collective-permute-start | bytes 786440 | tf_op jit(solution)/shard_map/while/body/eval_jaxpr/ppermute | solution.py:16
  293.8 78.0 %copy-start.6 = (bf16[512,512]{1,0:T(8,128)(2,1)S(1)}, bf16[512,512]{1,0:T(8,128)(2,1)}, u32[]{:S(2)}) copy-start(bf16[512,512]{1,0:T(8,128)(2,1)} %param.17) | copy-start | bytes 1572868
Sparse Core Ops, SparseCore 0:
  9.1 35.9 all-gather.1
  294.0 77.8 reduce-scatter.1
where the time goes:
time: 383 us; the launch traced here: 381 us
  waiting for transfers between devices  165 us (43%)
  starting transfers between devices  81.6 us (21%)
  local copies, waits for them, and re-layouts  52.5 us (14%)
  matrix products  49.2 us (13%)
  other arithmetic  18.6 us (5%)
  between operations  13.7 us (4%)
    ppermute x16, starting transfers between devices, from_behind(): return lax.ppermute(block, axis, route)  81.5 us
    reduce_scatter x1, waiting for transfers between devices, on_device(): lax.psum_scatter(partial_terms, 'tp', scatter_dimension=1, tiled=True)  78 us
    ppermute x16, waiting for transfers between devices, from_behind(): return lax.ppermute(block, axis, route)  58.9 us
    dynamic_update_slice x4, local copies, waits for them, and re-layouts, run_blocks(): lax.scan(block_step, (memory, start_total), (in_blocks(values), in_blocks...  30 us
    all_gather x1, waiting for transfers between devices, on_device(): gathered = lax.all_gather(hidden, 'tp', axis=1, tiled=True)  26.9 us
    unnamed x38, local copies, waits for them, and re-layouts  11.6 us
    dot_general x4, matrix products, block_step(): within = jnp.einsum('hts,shp->thp', scores, scaled, precision=PRECISE)  8.54 us
    dot_general x1, matrix products, on_device(): jnp.dot(mixed_rows, out_weight, preferred_element_type=jnp.float32)  8 us
  transfers between devices with their start and end apart: 18, of which 17 were waited for; matrix products, arithmetic and copies ran while one was open for 3% of the time, Pallas kernels for 0%

commit v1 on v0

--- a/solution.py
+++ b/solution.py
@@ -35,7 +35,7 @@
     row_pos = lax.broadcasted_iota(jnp.int32, (length, length), 0)
     col_pos = lax.broadcasted_iota(jnp.int32, (length, length), 1)
     causal = row_pos >= col_pos
-    cumulative = jnp.cumsum(log_decay, axis=0)
+    cumulative = jnp.dot(causal.astype(jnp.float32), log_decay, precision=PRECISE)
     across = cumulative.T
     spread = across[:, :, None] - across[:, None, :]
     weights = jnp.where(causal[None], jnp.exp(jnp.where(causal[None], spread, 0.0)), 0.0)

time: 383 us -> 379 us (0.990)
    unnamed x38 -> x46, local copies, waits for them, and re-layouts: 11.6 us -> 11.7 us
  transfers between devices with their start and end apart: 18 -> 18, of which waited for: 17 -> 17; matrix products, arithmetic and copies ran while one was open for 3% -> 4% of each run, Pallas kernels for 0% -> 0%
where the time goes in v1:
time: 379 us; the launch traced here: 377 us
  waiting for transfers between devices  164 us (43%)
  starting transfers between devices  81.6 us (22%)
  local copies, waits for them, and re-layouts  51.2 us (14%)
  matrix products  49.7 us (13%)
  other arithmetic  16.5 us (4%)
  between operations  13.8 us (4%)
    ppermute x16, starting transfers between devices, from_behind(): return lax.ppermute(block, axis, route)  81.6 us
    reduce_scatter x1, waiting for transfers between devices, on_device(): lax.psum_scatter(partial_terms, 'tp', scatter_dimension=1, tiled=True)  78 us
    ppermute x16, waiting for transfers between devices, from_behind(): return lax.ppermute(block, axis, route)  58.8 us
    dynamic_update_slice x4, local copies, waits for them, and re-layouts, run_blocks(): lax.scan(block_step, (memory, start_total), (in_blocks(values), in_blocks...  30.1 us
    all_gather x1, waiting for transfers between devices, on_device(): gathered = lax.all_gather(hidden, 'tp', axis=1, tiled=True)  26.4 us
    unnamed x46, local copies, waits for them, and re-layouts  11.7 us
    dot_general x4, matrix products, block_step(): within = jnp.einsum('hts,shp->thp', scores, scaled, precision=PRECISE)  8.54 us
    dot_general x1, matrix products, on_device(): jnp.dot(mixed_rows, out_weight, preferred_element_type=jnp.float32)  8.01 us
  transfers between devices with their start and end apart: 18, of which 17 were waited for; matrix products, arithmetic and copies ran while one was open for 4% of the time, Pallas kernels for 0%

profile of v1, /device:TPU:1, one launch (start us, length us, event | category | flops | bytes accessed | tf_op | source)
XLA Modules:
  0.0 377.3 jit_solution(4719193981872853301)
XLA Ops:
  8.1 9.4 %copy.69 = bf16[512,8,2,512]{3,1,2,0:T(8,128)(2,1)} copy(bf16[512,8,2,512]{3,2,1,0:T(2,128)(2,1)} %bitcast.152) | data formatting | bytes 16777216
  18.7 26.4 %all-gather.2.cloned.1.call-done = bf16[512,4096]{1,0:T(8,128)(2,1)} async-done(((bf16[512,512]{1,0:T(8,128)(2,1)}), bf16[512,4096]{1,0:T(8,128)(2,1)}) %all-gather.2.cloned.1.call-update) | async-done | bytes 4194320 | tf_op jit(solution)/shard_map/all_gather | solution.py:101
  45.0 3.2 fusion.36
  48.5 7.2 %convolution_convert_fusion = bf16[512,1024]{1,0:T(8,128)(2,1)S(1)} fusion(bf16[4096,1024]{1,0:T(8,128)(2,1)} %bitcast.153, bf16[512,4096]{1,0:T(8,128)(2,1)S(1)} %copy-done.3, f32[4096]{0:T(1024)S(1)} %convert_element_type.121, f32[512]{0:T(512)S(1)} %add_rsqrt_fusion.1), kind=kOutput, calls=%fused_computation.60 | convolution fusion | flops 4303880192 | bytes 13649920 | tf_op jit(solution)/shard_map/dot_general | solution.py:116
  56.6 4.3 %fusion.53 = bf16[512,256]{1,0:T(8,128)(2,1)S(1)} fusion(bf16[512,8,2,128]{3,2,1,0:T(2,128)(2,1)} %bitcast.168, bf16[512,4096]{1,0:T(8,128)(2,1)} %all-gather.2.cloned.1.call-done, f32[4096]{0:T(1024)S(1)} %convert_element_type.121, f32[512]{0:T(512)S(1)} %add_rsqrt_fusion.1), kind=kOutput, calls=%fused_computation.66 | convolution fusion | flops 1082261504 | bytes 6572032 | tf_op jit(solution)/shard_map/dot_general | solution.py:124
  61.0 3.2 collective-permute-start.1
  74.9 58.5 %while.28 = (s32[]{:T(128)}, f32[8,64,128]{2,1,0:T(8,128)S(1)}, f32[8]{0:T(128)S(1)}, f32[4,128,8,64]{1,0,3,2:T(4,128)}, f32[4,128,8]{1,2,0:T(8,128)S(1)}, /*ind...) while((s32[]{:T(128)}, f32[8,64,128]{2,1,0:T(8,128)S(1)}, ...), condition=%wide.region_2.3_spmd.clone, body=%wide.region_1.2_spmd.clone.sunk | while | flops 309004288 | bytes 3242933 | solution.py:70
  80.4 7.5 %dynamic_update_slice.14 = f32[4,128,8,64]{1,0,3,2:T(4,128)} dynamic-update-slice(f32[4,128,8,64]{1,0,3,2:T(4,128)} %get-tuple-element.343, f32[1,128,8,64]{1,0,3,2:T(1,128)S(1)} %bitcast.151, s32[]{:T(128)} %get-tuple-element.340, s32[]{:T(128)} %constant.28.clone.1..sunk, s32[]{:T(128)} %constant.28.clone.1..sunk, s32[]{:T(128)} %constant.28.clone.1..sunk) | dynamic-update-slice | bytes 524292 | tf_op jit(solution)/shard_map/while/body/jit(dynamic_update_index_in_dim)/dynamic_update_slice | solution.py:70
  95.0 7.5 %dynamic_update_slice.14 = f32[4,128,8,64]{1,0,3,2:T(4,128)} dynamic-update-slice(f32[4,128,8,64]{1,0,3,2:T(4,128)} %get-tuple-element.343, f32[1,128,8,64]{1,0,3,2:T(1,128)S(1)} %bitcast.151, s32[]{:T(128)} %get-tuple-element.340, s32[]{:T(128)} %constant.28.clone.1..sunk, s32[]{:T(128)} %constant.28.clone.1..sunk, s32[]{:T(128)} %constant.28.clone.1..sunk) | dynamic-update-slice | bytes 524292 | tf_op jit(solution)/shard_map/while/body/jit(dynamic_update_index_in_dim)/dynamic_update_slice | solution.py:70
  109.7 7.5 %dynamic_update_slice.14 = f32[4,128,8,64]{1,0,3,2:T(4,128)} dynamic-update-slice(f32[4,128,8,64]{1,0,3,2:T(4,128)} %get-tuple-element.343, f32[1,128,8,64]{1,0,3,2:T(1,128)S(1)} %bitcast.151, s32[]{:T(128)} %get-tuple-element.340, s32[]{:T(128)} %constant.28.clone.1..sunk, s32[]{:T(128)} %constant.28.clone.1..sunk, s32[]{:T(128)} %constant.28.clone.1..sunk) | dynamic-update-slice | bytes 524292 | tf_op jit(solution)/shard_map/while/body/jit(dynamic_update_index_in_dim)/dynamic_update_slice | solution.py:70
  119.9 2.1 convolution_bitcast_fusion.3
  124.3 7.5 %dynamic_update_slice.14 = f32[4,128,8,64]{1,0,3,2:T(4,128)} dynamic-update-slice(f32[4,128,8,64]{1,0,3,2:T(4,128)} %get-tuple-element.343, f32[1,128,8,64]{1,0,3,2:T(1,128)S(1)} %bitcast.151, s32[]{:T(128)} %get-tuple-element.340, s32[]{:T(128)} %constant.28.clone.1..sunk, s32[]{:T(128)} %constant.28.clone.1..sunk, s32[]{:T(128)} %constant.28.clone.1..sunk) | dynamic-update-slice | bytes 524292 | tf_op jit(solution)/shard_map/while/body/jit(dynamic_update_index_in_dim)/dynamic_update_slice | solution.py:70
  133.4 2.7 reshape.146
  136.1 139.5 %while.27 = (s32[]{:T(128)}, f32[8,64,128]{2,1,0:T(8,128)S(1)}, f32[8]{0:T(128)S(1)}, f32[8,64,128]{2,1,0:T(8,128)S(1)}, f32[]{:T(128)}, /*index=5*/f32[8,64,128]{2,1,0:T(8,128)S(1)}, s32[]{:T(128)}) while((s32[]{:T(128)}, f32[8,64,128]{2,1,0:T(8,128)S(1)}, f32[8]{0:T(128)S(1)}, f32[8,64,128]{2,1,0:T(8,128)S(1)}, f32[]{:T(128)}, ...), condition=%wide.region_4.5_spmd, body=%wide.region_3.4_spmd.sunk | while | flops 262146 | bytes 2621593 | solution.py:159
  136.2 3.3 collective-permute-start
  139.5 5.1 %collective-permute-done = f32[8,64,128]{2,1,0:T(8,128)S(1)} collective-permute-done((f32[8,64,128]{2,1,0:T(8,128)S(1)}, f32[8,64,128]{2,1,0:T(8,128)S(1)}, u32[]{:S(2)}, u32[]{:S(2)}) %collective-permute-start) | collective-permute-done | bytes 262176 | tf_op jit(solution)/shard_map/while/body/eval_jaxpr/ppermute | solution.py:16
  144.7 4.1 %collective-permute-start = (f32[8,64,128]{2,1,0:T(8,128)S(1)}, f32[8,64,128]{2,1,0:T(8,128)S(1)}, u32[]{:S(2)}, u32[]{:S(2)}) collective-permute-start(f32[8,64,128]{2,1,0:T(8,128)S(1)} %multiply_add_fusion.4), channel_id=1, source_target_pairs={{0,8},{8,16},{16,24},{24,32},{32,40},{40,48},{48,56},{56,64},{64,7... | collective-permute-start | bytes 786440 | tf_op jit(solution)/shard_map/while/body/eval_jaxpr/ppermute | solution.py:16
  148.8 4.2 %collective-permute-done = f32[8,64,128]{2,1,0:T(8,128)S(1)} collective-permute-done((f32[8,64,128]{2,1,0:T(8,128)S(1)}, f32[8,64,128]{2,1,0:T(8,128)S(1)}, u32[]{:S(2)}, u32[]{:S(2)}) %collective-permute-start) | collective-permute-done | bytes 262176 | tf_op jit(solution)/shard_map/while/body/eval_jaxpr/ppermute | solution.py:16
  153.1 4.1 %collective-permute-start = (f32[8,64,128]{2,1,0:T(8,128)S(1)}, f32[8,64,128]{2,1,0:T(8,128)S(1)}, u32[]{:S(2)}, u32[]{:S(2)}) collective-permute-start(f32[8,64,128]{2,1,0:T(8,128)S(1)} %multiply_add_fusion.4), channel_id=1, source_target_pairs={{0,8},{8,16},{16,24},{24,32},{32,40},{40,48},{48,56},{56,64},{64,7... | collective-permute-start | bytes 786440 | tf_op jit(solution)/shard_map/while/body/eval_jaxpr/ppermute | solution.py:16
  157.3 3.3 collective-permute-done
  160.7 3.8 %collective-permute-start = (f32[8,64,128]{2,1,0:T(8,128)S(1)}, f32[8,64,128]{2,1,0:T(8,128)S(1)}, u32[]{:S(2)}, u32[]{:S(2)}) collective-permute-start(f32[8,64,128]{2,1,0:T(8,128)S(1)} %multiply_add_fusion.4), channel_id=1, source_target_pairs={{0,8},{8,16},{16,24},{24,32},{32,40},{40,48},{48,56},{56,64},{64,7... | collective-permute-start | bytes 786440 | tf_op jit(solution)/shard_map/while/body/eval_jaxpr/ppermute | solution.py:16
  164.5 3.3 collective-permute-done
  168.0 3.8 %collective-permute-start = (f32[8,64,128]{2,1,0:T(8,128)S(1)}, f32[8,64,128]{2,1,0:T(8,128)S(1)}, u32[]{:S(2)}, u32[]{:S(2)}) collective-permute-start(f32[8,64,128]{2,1,0:T(8,128)S(1)} %multiply_add_fusion.4), channel_id=1, source_target_pairs={{0,8},{8,16},{16,24},{24,32},{32,40},{40,48},{48,56},{56,64},{64,7... | collective-permute-start | bytes 786440 | tf_op jit(solution)/shard_map/while/body/eval_jaxpr/ppermute | solution.py:16
  171.8 3.3 collective-permute-done
  175.2 4.1 %collective-permute-start = (f32[8,64,128]{2,1,0:T(8,128)S(1)}, f32[8,64,128]{2,1,0:T(8,128)S(1)}, u32[]{:S(2)}, u32[]{:S(2)}) collective-permute-start(f32[8,64,128]{2,1,0:T(8,128)S(1)} %multiply_add_fusion.4), channel_id=1, source_target_pairs={{0,8},{8,16},{16,24},{24,32},{32,40},{40,48},{48,56},{56,64},{64,7... | collective-permute-start | bytes 786440 | tf_op jit(solution)/shard_map/while/body/eval_jaxpr/ppermute | solution.py:16
  179.3 3.7 collective-permute-done
  183.1 5.6 %collective-permute-start = (f32[8,64,128]{2,1,0:T(8,128)S(1)}, f32[8,64,128]{2,1,0:T(8,128)S(1)}, u32[]{:S(2)}, u32[]{:S(2)}) collective-permute-start(f32[8,64,128]{2,1,0:T(8,128)S(1)} %multiply_add_fusion.4), channel_id=1, source_target_pairs={{0,8},{8,16},{16,24},{24,32},{32,40},{40,48},{48,56},{56,64},{64,7... | collective-permute-start | bytes 786440 | tf_op jit(solution)/shard_map/while/body/eval_jaxpr/ppermute | solution.py:16
  188.7 3.3 collective-permute-done
  192.1 6.2 %collective-permute-start = (f32[8,64,128]{2,1,0:T(8,128)S(1)}, f32[8,64,128]{2,1,0:T(8,128)S(1)}, u32[]{:S(2)}, u32[]{:S(2)}) collective-permute-start(f32[8,64,128]{2,1,0:T(8,128)S(1)} %multiply_add_fusion.4), channel_id=1, source_target_pairs={{0,8},{8,16},{16,24},{24,32},{32,40},{40,48},{48,56},{56,64},{64,7... | collective-permute-start | bytes 786440 | tf_op jit(solution)/shard_map/while/body/eval_jaxpr/ppermute | solution.py:16
  198.3 4.3 %collective-permute-done = f32[8,64,128]{2,1,0:T(8,128)S(1)} collective-permute-done((f32[8,64,128]{2,1,0:T(8,128)S(1)}, f32[8,64,128]{2,1,0:T(8,128)S(1)}, u32[]{:S(2)}, u32[]{:S(2)}) %collective-permute-start) | collective-permute-done | bytes 262176 | tf_op jit(solution)/shard_map/while/body/eval_jaxpr/ppermute | solution.py:16
  202.8 6.5 %collective-permute-start = (f32[8,64,128]{2,1,0:T(8,128)S(1)}, f32[8,64,128]{2,1,0:T(8,128)S(1)}, u32[]{:S(2)}, u32[]{:S(2)}) collective-permute-start(f32[8,64,128]{2,1,0:T(8,128)S(1)} %multiply_add_fusion.4), channel_id=1, source_target_pairs={{0,8},{8,16},{16,24},{24,32},{32,40},{40,48},{48,56},{56,64},{64,7... | collective-permute-start | bytes 786440 | tf_op jit(solution)/shard_map/while/body/eval_jaxpr/ppermute | solution.py:16
  209.3 5.4 %collective-permute-done = f32[8,64,128]{2,1,0:T(8,128)S(1)} collective-permute-done((f32[8,64,128]{2,1,0:T(8,128)S(1)}, f32[8,64,128]{2,1,0:T(8,128)S(1)}, u32[]{:S(2)}, u32[]{:S(2)}) %collective-permute-start) | collective-permute-done | bytes 262176 | tf_op jit(solution)/shard_map/while/body/eval_jaxpr/ppermute | solution.py:16
  214.9 6.9 %collective-permute-start = (f32[8,64,128]{2,1,0:T(8,128)S(1)}, f32[8,64,128]{2,1,0:T(8,128)S(1)}, u32[]{:S(2)}, u32[]{:S(2)}) collective-permute-start(f32[8,64,128]{2,1,0:T(8,128)S(1)} %multiply_add_fusion.4), channel_id=1, source_target_pairs={{0,8},{8,16},{16,24},{24,32},{32,40},{40,48},{48,56},{56,64},{64,7... | collective-permute-start | bytes 786440 | tf_op jit(solution)/shard_map/while/body/eval_jaxpr/ppermute | solution.py:16
  221.7 5.5 %collective-permute-done = f32[8,64,128]{2,1,0:T(8,128)S(1)} collective-permute-done((f32[8,64,128]{2,1,0:T(8,128)S(1)}, f32[8,64,128]{2,1,0:T(8,128)S(1)}, u32[]{:S(2)}, u32[]{:S(2)}) %collective-permute-start) | collective-permute-done | bytes 262176 | tf_op jit(solution)/shard_map/while/body/eval_jaxpr/ppermute | solution.py:16
  227.4 6.3 %collective-permute-start = (f32[8,64,128]{2,1,0:T(8,128)S(1)}, f32[8,64,128]{2,1,0:T(8,128)S(1)}, u32[]{:S(2)}, u32[]{:S(2)}) collective-permute-start(f32[8,64,128]{2,1,0:T(8,128)S(1)} %multiply_add_fusion.4), channel_id=1, source_target_pairs={{0,8},{8,16},{16,24},{24,32},{32,40},{40,48},{48,56},{56,64},{64,7... | collective-permute-start | bytes 786440 | tf_op jit(solution)/shard_map/while/body/eval_jaxpr/ppermute | solution.py:16
  233.8 4.4 %collective-permute-done = f32[8,64,128]{2,1,0:T(8,128)S(1)} collective-permute-done((f32[8,64,128]{2,1,0:T(8,128)S(1)}, f32[8,64,128]{2,1,0:T(8,128)S(1)}, u32[]{:S(2)}, u32[]{:S(2)}) %collective-permute-start) | collective-permute-done | bytes 262176 | tf_op jit(solution)/shard_map/while/body/eval_jaxpr/ppermute | solution.py:16
  238.3 4.9 %collective-permute-start = (f32[8,64,128]{2,1,0:T(8,128)S(1)}, f32[8,64,128]{2,1,0:T(8,128)S(1)}, u32[]{:S(2)}, u32[]{:S(2)}) collective-permute-start(f32[8,64,128]{2,1,0:T(8,128)S(1)} %multiply_add_fusion.4), channel_id=1, source_target_pairs={{0,8},{8,16},{16,24},{24,32},{32,40},{40,48},{48,56},{56,64},{64,7... | collective-permute-start | bytes 786440 | tf_op jit(solution)/shard_map/while/body/eval_jaxpr/ppermute | solution.py:16
  243.3 3.3 collective-permute-done
  246.7 6.2 %collective-permute-start = (f32[8,64,128]{2,1,0:T(8,128)S(1)}, f32[8,64,128]{2,1,0:T(8,128)S(1)}, u32[]{:S(2)}, u32[]{:S(2)}) collective-permute-start(f32[8,64,128]{2,1,0:T(8,128)S(1)} %multiply_add_fusion.4), channel_id=1, source_target_pairs={{0,8},{8,16},{16,24},{24,32},{32,40},{40,48},{48,56},{56,64},{64,7... | collective-permute-start | bytes 786440 | tf_op jit(solution)/shard_map/while/body/eval_jaxpr/ppermute | solution.py:16
  252.9 3.3 collective-permute-done
  256.3 6.2 %collective-permute-start = (f32[8,64,128]{2,1,0:T(8,128)S(1)}, f32[8,64,128]{2,1,0:T(8,128)S(1)}, u32[]{:S(2)}, u32[]{:S(2)}) collective-permute-start(f32[8,64,128]{2,1,0:T(8,128)S(1)} %multiply_add_fusion.4), channel_id=1, source_target_pairs={{0,8},{8,16},{16,24},{24,32},{32,40},{40,48},{48,56},{56,64},{64,7... | collective-permute-start | bytes 786440 | tf_op jit(solution)/shard_map/while/body/eval_jaxpr/ppermute | solution.py:16
  262.6 3.3 collective-permute-done
  266.0 6.2 %collective-permute-start = (f32[8,64,128]{2,1,0:T(8,128)S(1)}, f32[8,64,128]{2,1,0:T(8,128)S(1)}, u32[]{:S(2)}, u32[]{:S(2)}) collective-permute-start(f32[8,64,128]{2,1,0:T(8,128)S(1)} %multiply_add_fusion.4), channel_id=1, source_target_pairs={{0,8},{8,16},{16,24},{24,32},{32,40},{40,48},{48,56},{56,64},{64,7... | collective-permute-start | bytes 786440 | tf_op jit(solution)/shard_map/while/body/eval_jaxpr/ppermute | solution.py:16
  272.3 3.3 collective-permute-done
  275.6 4.7 %fusion.50 = f32[512,8,64]{0,2,1:T(8,128)} fusion(f32[512,8,64]{0,2,1:T(8,128)} %reshape.146, f32[8,64,128]{2,1,0:T(8,128)S(1)} %get-tuple-element.95, f32[512,8,64]{0,2,1:T(8,128)S(1)} %bitcast.156, f32[512,8]{0,1:T(8,128)S(1)} %exponential_bitcast_fusion, f32[512,128]{1,0:T(8,128)S(1)} %copy-done.7, f32[8]{0:T(128)S(1)} %copy-done.18), kind=kOutput, calls=%fused_computation.63 | convolution fusion | flops 403963904 | bytes 3686432 | tf_op jit(solution)/shard_map/thn,hpn->thp/dot_general | solution.py:161
  282.3 8.0 %fusion.67 = f32[512,4096]{1,0:T(8,128)} fusion(bf16[512,4096]{1,0:T(8,128)(2,1)} %param.28, f32[512]{0:T(512)S(1)} %convert_element_type.146, f32[512]{0:T(512)S(1)} %add_rsqrt_fusion, f32[512,1,512]{2,0,1:T(8,128)S(1)} %copy.56, bf16[512,1,512]{2,0,1:T(8,128)(2,1)S(1)} %copy.62), kind=kOutput, calls=%fused_computation.85 | convolution fusion | flops 2149842944 | bytes 14159872 | tf_op jit(solution)/shard_map/dot_general | solution.py:173
  290.3 78.0 %reduce-scatter.2.cloned.1.call-done = f32[512,512]{1,0:T(8,128)} async-done(((f32[512,4096]{1,0:T(8,128)}), f32[512,512]{1,0:T(8,128)}) %reduce-scatter.2.cloned.1.call-update) | async-done | bytes 1048592 | tf_op jit(solution)/shard_map/reduce_scatter | solution.py:174
  368.3 2.2 add_convert_fusion
  (159 shorter events, 44.2 us)
Async XLA Ops:
  6.5 57.7 %copy-start = (bf16[4096,8]{0,1:T(8,128)(2,1)S(1)}, bf16[4096,8]{0,1:T(8,128)(2,1)}, u32[]{:S(2)}) copy-start(bf16[4096,8]{0,1:T(8,128)(2,1)} %param.21) | copy-start | bytes 196612
  6.5 38.5 %all-gather.2.cloned.1.call-start = ((), (), s32[]{:S(2)}) async-start(), calls=%async_computation.1 | async-start | bytes 4718592 | tf_op jit(solution)/shard_map/all_gather | solution.py:101
  7.3 361.1 %reduce-scatter.2.cloned.1.call-start = ((), (), s32[]{:S(2)}) async-start(), calls=%async_computation.2 | async-start | bytes 9437184 | tf_op jit(solution)/shard_map/reduce_scatter | solution.py:174
  8.0 9.4 %copy-start.19 = (f32[8]{0:T(128)S(1)}, f32[8]{0:T(128)}, u32[]{:S(2)}) copy-start(f32[8]{0:T(128)} %param.25) | copy-start | bytes 100
  8.1 10.0 %copy-start.16 = (bf16[512]{0:T(512)(128)(2,1)S(1)}, bf16[512]{0:T(512)(128)(2,1)}, u32[]{:S(2)}) copy-start(bf16[512]{0:T(512)(128)(2,1)} %param.27) | copy-start | bytes 3076
  8.1 10.0 %copy-start.14 = (bf16[4,2,128]{2,1,0:T(2,128)(2,1)S(1)}, bf16[4,2,128]{2,1,0:T(2,128)(2,1)}, u32[]{:S(2)}) copy-start(bf16[4,2,128]{2,1,0:T(2,128)(2,1)} %param.23) | copy-start | bytes 6148
  8.1 10.6 %copy-start.9 = (bf16[4,512]{1,0:T(4,128)(2,1)S(1)}, bf16[4,512]{1,0:T(4,128)(2,1)}, u32[]{:S(2)}) copy-start(bf16[4,512]{1,0:T(4,128)(2,1)} %param.22) | copy-start | bytes 12292
  8.1 10.6 %copy-start.1 = (f32[8,64,128]{2,1,0:T(8,128)S(1)}, f32[8,64,128]{2,1,0:T(8,128)}, u32[]{:S(2)}) copy-start(f32[8,64,128]{2,1,0:T(8,128)} %param.29) | copy-start | bytes 786436
  45.0 3.4 copy-start.3
  48.3 8.3 %copy-start.15 = (f32[512]{0:T(512)}, f32[512]{0:T(512)S(1)}, u32[]{:S(2)}) copy-start(f32[512]{0:T(512)S(1)} %add_rsqrt_fusion.1) | copy-start | bytes 6148
  56.5 7.7 %copy-start.4 = (bf16[512,4096]{1,0:T(8,128)(2,1)S(1)}, bf16[512,4096]{1,0:T(8,128)(2,1)}, u32[]{:S(2)}) copy-start(bf16[512,4096]{1,0:T(8,128)(2,1)} %all-gather.2.cloned.1.call-done) | copy-start | bytes 12582916
  56.5 7.7 %copy-start.20 = (f32[8]{0:T(128)S(1)}, f32[8]{0:T(128)}, u32[]{:S(2)}) copy-start(f32[8]{0:T(128)} %param.24) | copy-start | bytes 100
  60.9 5.3 %copy-start.8 = (bf16[512,256]{1,0:T(8,128)(2,1)}, bf16[512,256]{1,0:T(8,128)(2,1)S(1)}, u32[]{:S(2)}) copy-start(bf16[512,256]{1,0:T(8,128)(2,1)S(1)} %fusion.53) | copy-start | bytes 786436
  61.0 5.3 %copy-start.17 = (f32[8]{0:T(128)S(1)}, f32[8]{0:T(128)}, u32[]{:S(2)}) copy-start(f32[8]{0:T(128)} %exp.52) | copy-start | bytes 100
  61.0 5.8 %collective-permute-start.1 = (bf16[3,768]{1,0:T(4,128)(2,1)S(1)}, bf16[3,768]{1,0:T(4,128)(2,1)S(1)}, u32[]{:S(2)}, u32[]{:S(2)}) collective-permute-start(bf16[3,768]{1,0:T(4,128)(2,1)S(1)} %pad_maximum_fusion.2), channel_id=1, source_target_pairs={{0,8},{8,16},{16,24},{24,32},{32,40},{40,48},{48,56},{56,64},{64,7... | collective-permute-start | bytes 13832 | tf_op jit(solution)/shard_map/ppermute | solution.py:16
  67.5 4.7 %copy-start.10 = (f32[2,128]{1,0:T(2,128)S(1)}, f32[2,128]{1,0:T(2,128)}, u32[]{:S(2)}) copy-start(f32[2,128]{1,0:T(2,128)} %get-tuple-element.212) | copy-start | bytes 3076
  67.5 4.7 %copy-start.11 = (f32[2,128]{1,0:T(2,128)S(1)}, f32[2,128]{1,0:T(2,128)}, u32[]{:S(2)}) copy-start(f32[2,128]{1,0:T(2,128)} %get-tuple-element.213) | copy-start | bytes 3076
  67.5 4.7 %copy-start.12 = (f32[2,128]{1,0:T(2,128)S(1)}, f32[2,128]{1,0:T(2,128)}, u32[]{:S(2)}) copy-start(f32[2,128]{1,0:T(2,128)} %get-tuple-element.214) | copy-start | bytes 3076
  67.5 4.7 %copy-start.13 = (f32[2,128]{1,0:T(2,128)S(1)}, f32[2,128]{1,0:T(2,128)}, u32[]{:S(2)}) copy-start(f32[2,128]{1,0:T(2,128)} %get-tuple-element.215) | copy-start | bytes 3076
  70.6 2.6 copy-start.2
  136.1 139.5 %copy-start.5 = (f32[512,512]{0,1:T(8,128)S(1)}, f32[512,512]{0,1:T(8,128)}, u32[]{:S(2)}) copy-start(f32[512,512]{0,1:T(8,128)} %copy.54) | copy-start | bytes 3145732
  136.1 139.5 %copy-start.7 = (f32[512,128]{1,0:T(8,128)S(1)}, f32[512,128]{1,0:T(8,128)}, u32[]{:S(2)}) copy-start(f32[512,128]{1,0:T(8,128)} %get-tuple-element.204) | copy-start | bytes 786436
  136.1 139.5 %copy-start.18 = (f32[8]{0:T(128)S(1)}, f32[8]{0:T(128)}, u32[]{:S(2)}) copy-start(f32[8]{0:T(128)} %param.26) | copy-start | bytes 100
  136.2 8.4 %collective-permute-start = (f32[8,64,128]{2,1,0:T(8,128)S(1)}, f32[8,64,128]{2,1,0:T(8,128)S(1)}, u32[]{:S(2)}, u32[]{:S(2)}) collective-permute-start(f32[8,64,128]{2,1,0:T(8,128)S(1)} %multiply_add_fusion.4), channel_id=1, source_target_pairs={{0,8},{8,16},{16,24},{24,32},{32,40},{40,48},{48,56},{56,64},{64,7... | collective-permute-start | bytes 786440 | tf_op jit(solution)/shard_map/while/body/eval_jaxpr/ppermute | solution.py:16
  144.7 8.3 %collective-permute-start = (f32[8,64,128]{2,1,0:T(8,128)S(1)}, f32[8,64,128]{2,1,0:T(8,128)S(1)}, u32[]{:S(2)}, u32[]{:S(2)}) collective-permute-start(f32[8,64,128]{2,1,0:T(8,128)S(1)} %multiply_add_fusion.4), channel_id=1, source_target_pairs={{0,8},{8,16},{16,24},{24,32},{32,40},{40,48},{48,56},{56,64},{64,7... | collective-permute-start | bytes 786440 | tf_op jit(solution)/shard_map/while/body/eval_jaxpr/ppermute | solution.py:16
  153.1 7.4 %collective-permute-start = (f32[8,64,128]{2,1,0:T(8,128)S(1)}, f32[8,64,128]{2,1,0:T(8,128)S(1)}, u32[]{:S(2)}, u32[]{:S(2)}) collective-permute-start(f32[8,64,128]{2,1,0:T(8,128)S(1)} %multiply_add_fusion.4), channel_id=1, source_target_pairs={{0,8},{8,16},{16,24},{24,32},{32,40},{40,48},{48,56},{56,64},{64,7... | collective-permute-start | bytes 786440 | tf_op jit(solution)/shard_map/while/body/eval_jaxpr/ppermute | solution.py:16
  160.7 7.1 %collective-permute-start = (f32[8,64,128]{2,1,0:T(8,128)S(1)}, f32[8,64,128]{2,1,0:T(8,128)S(1)}, u32[]{:S(2)}, u32[]{:S(2)}) collective-permute-start(f32[8,64,128]{2,1,0:T(8,128)S(1)} %multiply_add_fusion.4), channel_id=1, source_target_pairs={{0,8},{8,16},{16,24},{24,32},{32,40},{40,48},{48,56},{56,64},{64,7... | collective-permute-start | bytes 786440 | tf_op jit(solution)/shard_map/while/body/eval_jaxpr/ppermute | solution.py:16
  168.0 7.1 %collective-permute-start = (f32[8,64,128]{2,1,0:T(8,128)S(1)}, f32[8,64,128]{2,1,0:T(8,128)S(1)}, u32[]{:S(2)}, u32[]{:S(2)}) collective-permute-start(f32[8,64,128]{2,1,0:T(8,128)S(1)} %multiply_add_fusion.4), channel_id=1, source_target_pairs={{0,8},{8,16},{16,24},{24,32},{32,40},{40,48},{48,56},{56,64},{64,7... | collective-permute-start | bytes 786440 | tf_op jit(solution)/shard_map/while/body/eval_jaxpr/ppermute | solution.py:16
  175.2 7.8 %collective-permute-start = (f32[8,64,128]{2,1,0:T(8,128)S(1)}, f32[8,64,128]{2,1,0:T(8,128)S(1)}, u32[]{:S(2)}, u32[]{:S(2)}) collective-permute-start(f32[8,64,128]{2,1,0:T(8,128)S(1)} %multiply_add_fusion.4), channel_id=1, source_target_pairs={{0,8},{8,16},{16,24},{24,32},{32,40},{40,48},{48,56},{56,64},{64,7... | collective-permute-start | bytes 786440 | tf_op jit(solution)/shard_map/while/body/eval_jaxpr/ppermute | solution.py:16
  183.1 8.8 %collective-permute-start = (f32[8,64,128]{2,1,0:T(8,128)S(1)}, f32[8,64,128]{2,1,0:T(8,128)S(1)}, u32[]{:S(2)}, u32[]{:S(2)}) collective-permute-start(f32[8,64,128]{2,1,0:T(8,128)S(1)} %multiply_add_fusion.4), channel_id=1, source_target_pairs={{0,8},{8,16},{16,24},{24,32},{32,40},{40,48},{48,56},{56,64},{64,7... | collective-permute-start | bytes 786440 | tf_op jit(solution)/shard_map/while/body/eval_jaxpr/ppermute | solution.py:16
  192.1 10.5 %collective-permute-start = (f32[8,64,128]{2,1,0:T(8,128)S(1)}, f32[8,64,128]{2,1,0:T(8,128)S(1)}, u32[]{:S(2)}, u32[]{:S(2)}) collective-permute-start(f32[8,64,128]{2,1,0:T(8,128)S(1)} %multiply_add_fusion.4), channel_id=1, source_target_pairs={{0,8},{8,16},{16,24},{24,32},{32,40},{40,48},{48,56},{56,64},{64,7... | collective-permute-start | bytes 786440 | tf_op jit(solution)/shard_map/while/body/eval_jaxpr/ppermute | solution.py:16
  202.8 11.9 %collective-permute-start = (f32[8,64,128]{2,1,0:T(8,128)S(1)}, f32[8,64,128]{2,1,0:T(8,128)S(1)}, u32[]{:S(2)}, u32[]{:S(2)}) collective-permute-start(f32[8,64,128]{2,1,0:T(8,128)S(1)} %multiply_add_fusion.4), channel_id=1, source_target_pairs={{0,8},{8,16},{16,24},{24,32},{32,40},{40,48},{48,56},{56,64},{64,7... | collective-permute-start | bytes 786440 | tf_op jit(solution)/shard_map/while/body/eval_jaxpr/ppermute | solution.py:16
  214.9 12.4 %collective-permute-start = (f32[8,64,128]{2,1,0:T(8,128)S(1)}, f32[8,64,128]{2,1,0:T(8,128)S(1)}, u32[]{:S(2)}, u32[]{:S(2)}) collective-permute-start(f32[8,64,128]{2,1,0:T(8,128)S(1)} %multiply_add_fusion.4), channel_id=1, source_target_pairs={{0,8},{8,16},{16,24},{24,32},{32,40},{40,48},{48,56},{56,64},{64,7... | collective-permute-start | bytes 786440 | tf_op jit(solution)/shard_map/while/body/eval_jaxpr/ppermute | solution.py:16
  227.4 10.7 %collective-permute-start = (f32[8,64,128]{2,1,0:T(8,128)S(1)}, f32[8,64,128]{2,1,0:T(8,128)S(1)}, u32[]{:S(2)}, u32[]{:S(2)}) collective-permute-start(f32[8,64,128]{2,1,0:T(8,128)S(1)} %multiply_add_fusion.4), channel_id=1, source_target_pairs={{0,8},{8,16},{16,24},{24,32},{32,40},{40,48},{48,56},{56,64},{64,7... | collective-permute-start | bytes 786440 | tf_op jit(solution)/shard_map/while/body/eval_jaxpr/ppermute | solution.py:16
  238.3 8.2 %collective-permute-start = (f32[8,64,128]{2,1,0:T(8,128)S(1)}, f32[8,64,128]{2,1,0:T(8,128)S(1)}, u32[]{:S(2)}, u32[]{:S(2)}) collective-permute-start(f32[8,64,128]{2,1,0:T(8,128)S(1)} %multiply_add_fusion.4), channel_id=1, source_target_pairs={{0,8},{8,16},{16,24},{24,32},{32,40},{40,48},{48,56},{56,64},{64,7... | collective-permute-start | bytes 786440 | tf_op jit(solution)/shard_map/while/body/eval_jaxpr/ppermute | solution.py:16
  246.7 9.5 %collective-permute-start = (f32[8,64,128]{2,1,0:T(8,128)S(1)}, f32[8,64,128]{2,1,0:T(8,128)S(1)}, u32[]{:S(2)}, u32[]{:S(2)}) collective-permute-start(f32[8,64,128]{2,1,0:T(8,128)S(1)} %multiply_add_fusion.4), channel_id=1, source_target_pairs={{0,8},{8,16},{16,24},{24,32},{32,40},{40,48},{48,56},{56,64},{64,7... | collective-permute-start | bytes 786440 | tf_op jit(solution)/shard_map/while/body/eval_jaxpr/ppermute | solution.py:16
  256.3 9.5 %collective-permute-start = (f32[8,64,128]{2,1,0:T(8,128)S(1)}, f32[8,64,128]{2,1,0:T(8,128)S(1)}, u32[]{:S(2)}, u32[]{:S(2)}) collective-permute-start(f32[8,64,128]{2,1,0:T(8,128)S(1)} %multiply_add_fusion.4), channel_id=1, source_target_pairs={{0,8},{8,16},{16,24},{24,32},{32,40},{40,48},{48,56},{56,64},{64,7... | collective-permute-start | bytes 786440 | tf_op jit(solution)/shard_map/while/body/eval_jaxpr/ppermute | solution.py:16
  266.0 9.5 %collective-permute-start = (f32[8,64,128]{2,1,0:T(8,128)S(1)}, f32[8,64,128]{2,1,0:T(8,128)S(1)}, u32[]{:S(2)}, u32[]{:S(2)}) collective-permute-start(f32[8,64,128]{2,1,0:T(8,128)S(1)} %multiply_add_fusion.4), channel_id=1, source_target_pairs={{0,8},{8,16},{16,24},{24,32},{32,40},{40,48},{48,56},{56,64},{64,7... | collective-permute-start | bytes 786440 | tf_op jit(solution)/shard_map/while/body/eval_jaxpr/ppermute | solution.py:16
  290.3 78.0 %copy-start.6 = (bf16[512,512]{1,0:T(8,128)(2,1)S(1)}, bf16[512,512]{1,0:T(8,128)(2,1)}, u32[]{:S(2)}) copy-start(bf16[512,512]{1,0:T(8,128)(2,1)} %param.17) | copy-start | bytes 1572868
Sparse Core Ops, SparseCore 0:
  9.1 35.9 all-gather.1
  290.5 77.8 reduce-scatter.1

commit v2 on v1

v2 whole, which is shorter than its diff:
```python
import functools

import jax
import jax.numpy as jnp
from jax import lax
from jax.experimental import pallas as pl
from jax.experimental.pallas import tpu as pltpu
from jax.sharding import PartitionSpec as P

F32 = jnp.float32
BF16 = jnp.bfloat16
EPSILON = 1e-05
MESH = pl.DeviceIdType.MESH
HIGHEST = lax.Precision.HIGHEST

ROWS = 512
FEAT = 512
MODEL = 4096
HEADS = 8
WIDTH = 64
STATE = 128
CHUNK = 128
NCHUNK = ROWS // CHUNK
HALF = CHUNK // 2
NSEQ = 16
NTP = 8
NCHIP = 4
COLS = 1408
RING_AG = 9
RING_RS = 8


def silu(v):
    return v / (1.0 + jnp.exp(-v))


def softplus(v):
    return jnp.maximum(v, 0.0) + jnp.log1p(jnp.exp(-jnp.abs(v)))


def dot(a, b, precision=None):
    return jnp.dot(a, b, preferred_element_type=F32, precision=precision)


def iota(shape, dim):
    return lax.broadcasted_iota(jnp.int32, shape, dim)


def across_heads(rows):
    lane = iota((1, 128), 1)
    parts = [
        jnp.where(lane < WIDTH, rows[2 * j : 2 * j + 1, :], rows[2 * j + 1 : 2 * j + 2, :])
        for j in range(4)
    ]
    return jnp.concatenate(parts, axis=1)


def kernel(
    hidden,
    gain_ref,
    gx_hbm,
    sw_hbm,
    stepw_ref,
    tap_x,
    tap_s,
    bias_ref,
    decay_ref,
    skip_ref,
    igain_ref,
    wo_hbm,
    init_ref,
    out_ref,
    gx_raw,
    sw_raw,
    w,
    wo,
    g,
    ss_send,
    ss_recv,
    rfull,
    xf,
    steps,
    sz,
    y,
    ec,
    sloc,
    pre,
    state,
    total_log,
    cmap,
    halo_send,
    halo_recv,
    piece_send,
    piece_recv,
    enter_send,
    enter_recv,
    init_t,
    entering,
    xs,
    xr,
    part,
    far_send,
    near_send,
    far_recv,
    near_recv,
    load_sem,
    ag_send,
    ag_recv,
    ss_ssem,
    ss_rsem,
    halo_ssem,
    halo_rsem,
    p_ssem,
    p_rsem,
    e_ssem,
    e_rsem,
    rs_ssem,
    rs_rsem,
):
    seq = lax.axis_index("seq")
    tp = lax.axis_index("tp")
    chip = tp // 2
    core = tp % 2
    up = (chip + 1) % NCHIP
    down = (chip + 3) % NCHIP
    far = (chip + 2) % NCHIP
    tp_up = up * 2 + core
    tp_down = down * 2 + core
    tp_far = far * 2 + core
    sibling = chip * 2 + (1 - core)

    loads = [
        pltpu.make_async_copy(gx_hbm, gx_raw, load_sem.at[0]),
        pltpu.make_async_copy(sw_hbm, sw_raw, load_sem.at[1]),
        pltpu.make_async_copy(wo_hbm, wo, load_sem.at[2]),
    ]
    for load in loads:
        load.start()

    barrier = pltpu.get_barrier_semaphore()

    @pl.loop(1, NTP)
    def _(k):
        pl.semaphore_signal(
            barrier, inc=1, device_id={"tp": (tp + k) % NTP}, device_id_type=MESH
        )

    @pl.loop(1, NSEQ)
    def _(k):
        pl.semaphore_signal(
            barrier, inc=1, device_id={"seq": (seq + k) % NSEQ}, device_id_type=MESH
        )

    gain_rows = gain_ref[...].astype(F32)
    gain_at = iota((MODEL // 128, 128), 0)
    gain = jnp.concatenate(
        [
            jnp.sum(jnp.where(gain_at == tp * 4 + j, gain_rows, 0.0), axis=0, keepdims=True)
            for j in range(4)
        ],
        axis=1,
    )
    own = pl.ds(pl.multiple_of(tp * FEAT, FEAT), FEAT)
    squares = []
    for c in range(NCHUNK):
        rows = slice(c * CHUNK, (c + 1) * CHUNK)
        h = hidden[rows, :].astype(F32)
        g[rows, own] = (h * gain).astype(BF16)
        summed = jnp.sum(h * h, axis=1, keepdims=True)
        squares.append(jnp.broadcast_to(summed, (CHUNK, 128)).T[0:1, :])
    ss_send[...] = jnp.concatenate(squares + [jnp.zeros((4, 128), F32)], axis=0)

    pl.semaphore_wait(barrier, NTP - 1 + NSEQ - 1)

    def ag_copy(step, kind):
        row = pl.multiple_of(((step + NCHUNK - 1) % NCHUNK) * CHUNK, CHUNK)
        whole, first, second = (row, CHUNK), (row, HALF), (pl.multiple_of(row + HALF, HALF), HALF)
        (start, size), shard, target = (
            (whole, tp, tp_up),
            (whole, tp, tp_down),
            (whole, tp, sibling),
            (first, tp_down, tp_up),
            (second, tp_up, tp_down),
            (whole, tp_down, sibling),
            (whole, tp_up, sibling),
            (first, tp_far, sibling),
            (second, tp_far, sibling),
        )[kind]
        block = g.at[pl.ds(start, size), pl.ds(pl.multiple_of(shard * FEAT, FEAT), FEAT)]
        return pltpu.make_async_remote_copy(
            src_ref=block,
            dst_ref=block,
            send_sem=ag_send.at[step, kind],
            recv_sem=ag_recv.at[step, kind],
            device_id={"tp": target},
            device_id_type=MESH,
        )

    def send_own(step):
        for kind in (0, 1, 2):
            ag_copy(step, kind).start()

    send_own(0)

    def ss_copy(k):
        return pltpu.make_async_remote_copy(
            src_ref=ss_send,
            dst_ref=ss_recv.at[tp],
            send_sem=ss_ssem.at[k],
            recv_sem=ss_rsem.at[k],
            device_id={"tp": (tp + k) % NTP},
            device_id_type=MESH,
        )

    @pl.loop(1, NTP)
    def _(k):
        ss_copy(k).start()

    ss_recv[tp] = ss_send[...]
    send_own(1)

    loads[0].wait()
    o256, i256 = iota((256, 256), 0), iota((256, 256), 1)
    pick = jnp.where(i256 == (o256 % 32) * 8 + o256 // 32, 1.0, 0.0).astype(BF16)

    @pl.loop(0, 64)
    def _(b):
        at = pl.multiple_of(b * 512, 512)
        k0 = pl.multiple_of(b * 64, 64)
        both = jnp.concatenate([gx_raw[pl.ds(at, 256), :], gx_raw[pl.ds(at + 256, 256), :]], axis=1)
        sorted_rows = dot(pick, both).astype(BF16)
        for m in range(8):
            column = (m % 2) * 512 + (m // 2) * 128
            rows = sorted_rows[m * 32 : (m + 1) * 32, :]
            w[pl.ds(k0, 32), column : column + 128] = rows[:, :128]
            w[pl.ds(k0 + 32, 32), column : column + 128] = rows[:, 128:]

    loads[1].wait()
    pick_state = jnp.where(i256 == (o256 % 128) * 2 + o256 // 128, 1.0, 0.0).astype(BF16)

    @pl.loop(0, 16)
    def _(b):
        at = pl.multiple_of(b * 512, 512)
        k0 = pl.multiple_of(b * 256, 256)
        both = jnp.concatenate([sw_raw[pl.ds(at, 256), :], sw_raw[pl.ds(at + 256, 256), :]], axis=1)
        sorted_rows = dot(pick_state, both).astype(BF16)
        for m in range(2):
            column = 1024 + m * 128
            rows = sorted_rows[m * 128 : (m + 1) * 128, :]
            w[pl.ds(k0, 128), column : column + 128] = rows[:, :128]
            w[pl.ds(k0 + 128, 128), column : column + 128] = rows[:, 128:]

    @pl.loop(0, 32)
    def _(b):
        at = pl.multiple_of(b * 128, 128)
        rows = stepw_ref[:, pl.ds(at, 128)].astype(F32)
        square = jnp.concatenate([rows, jnp.zeros((120, 128), F32)], axis=0)
        w[pl.ds(at, 128), 1280:1408] = square.T.astype(BF16)

    for j in range(4):
        init_t[:, j * 128 : (j + 1) * 128] = init_ref[j * 128 : (j + 1) * 128, :].T

    lane512 = iota((1, 512), 1)
    row8 = iota((8, 128), 0)
    bias = jnp.zeros((8, 128), F32)
    rate = jnp.zeros((8, 128), F32)
    skip = jnp.zeros((1, 512), F32)
    for h in range(HEADS):
        bias = jnp.where(row8 == h, bias_ref[h], bias)
        rate = jnp.where(row8 == h, decay_ref[h], rate)
        skip = jnp.where(lane512 // WIDTH == h, skip_ref[h], skip)
    rate = jnp.exp(rate)
    r128, c128 = iota((128, 128), 0), iota((128, 128), 1)
    causal = r128 >= c128
    upper = jnp.where(r128 <= c128, 1.0, 0.0)
    s_row, s_lane = iota((128, 512), 0), iota((128, 512), 1)
    spread_decay = jnp.where(s_row == HEADS + s_lane // WIDTH, 1.0, 0.0).astype(BF16)
    spread_step = jnp.where(s_row == 2 * HEADS + s_lane // WIDTH, 1.0, 0.0).astype(BF16)

    state[...] = jnp.zeros((STATE, FEAT), F32)
    total_log[...] = jnp.zeros((8, 128), F32)

    halo_copy = pltpu.make_async_remote_copy(
        src_ref=halo_send,
        dst_ref=halo_recv,
        send_sem=halo_ssem,
        recv_sem=halo_rsem,
        device_id={"seq": (seq + 1) % NSEQ},
        device_id_type=MESH,
    )

    def project(step):
        row = pl.multiple_of(((step + NCHUNK - 1) % NCHUNK) * CHUNK, CHUNK)
        rows = pl.ds(row, CHUNK)
        r = rfull[rows, :]
        r2 = jnp.concatenate([r, r], axis=1)

        @pl.loop(0, 2)
        def _(n):
            cols = pl.ds(pl.multiple_of(n * 256, 256), 256)
            z = (dot(g[rows, :], w[:, cols]) * r2).astype(BF16).astype(F32)
            sz[rows, cols] = silu(z)

        @pl.loop(0, 3)
        def _(n):
            at = pl.multiple_of(n * 256, 256)
            raw = (dot(g[rows, :], w[:, pl.ds(pl.multiple_of(at + 512, 256), 256)]) * r2).astype(BF16)
            xf[pl.ds(pl.multiple_of(row + 16, 16), CHUNK), pl.ds(at, 256)] = raw.astype(F32)

        raw_step = (dot(g[rows, :], w[:, 1280:1408]) * r).astype(BF16).astype(F32)
        steps[:, rows] = raw_step.T[0:HEADS, :]

    def scan_chunk(c):
        row = pl.multiple_of(c * CHUNK, CHUNK)
        rows = pl.ds(row, CHUNK)

        def filtered(cols, taps):
            padded = xf[pl.ds(pl.multiple_of(row + 8, 8), CHUNK + 8), cols]
            summed = taps[0] * padded[5 : 5 + CHUNK]
            for k in range(1, 4):
                summed = summed + taps[k] * padded[5 + k : 5 + k + CHUNK]
            return silu(summed).astype(BF16)

        taps_x = tap_x[...].astype(F32)
        taps_s = tap_s[...].astype(F32)
        values = jnp.concatenate(
            [
                filtered(
                    slice(j * 128, (j + 1) * 128),
                    [taps_x[k : k + 1, j * 128 : (j + 1) * 128] for k in range(4)],
                )
                for j in range(4)
            ],
            axis=1,
        )
        in_map, out_map = (
            filtered(
                slice(512 + m * 128, 640 + m * 128),
                [taps_s[2 * k + m : 2 * k + m + 1, :] for k in range(4)],
            )
            for m in range(2)
        )
        cmap[rows, :] = out_map
        in_map_t = in_map.astype(F32).T.astype(BF16)
        step = softplus(steps[:, rows] + bias)
        cum = dot(-step * rate, upper, HIGHEST)
        last = jnp.broadcast_to(cum[:, 127:128], (8, 128))
        kept = step * jnp.exp(last - cum)
        columns = jnp.concatenate(
            [cum, jnp.exp(cum), kept, jnp.zeros((104, 128), F32)], axis=0
        ).T
        high = columns.astype(BF16)
        low = (columns - high.astype(F32)).astype(BF16)
        decay_exp = dot(high, spread_decay) + dot(low, spread_decay)
        step_exp = dot(high, spread_step) + dot(low, spread_step)
        ec[rows, :] = decay_exp
        wide = values.astype(F32)
        weighted = (wide * step_exp).astype(BF16)
        before = state[...]
        sloc[c] = before
        pre[c] = jnp.broadcast_to(jnp.exp(across_heads(total_log[...])), (8, FEAT))
        total_log[...] += last
        state[...] = jnp.exp(across_heads(last)) * before + dot(in_map_t, weighted)

        scores = dot(out_map, in_map_t)
        lane = iota((CHUNK, 128), 1)
        for j in range(4):
            pair = values[:, j * 128 : (j + 1) * 128]
            both = []
            for h in (2 * j, 2 * j + 1):
                spread = columns[:, h : h + 1] - cum[h : h + 1, :]
                weights = jnp.exp(jnp.where(causal, spread, -1e30))
                both.append(dot((scores * weights * step[h : h + 1, :]).astype(BF16), pair))
            cols = slice(j * 128, (j + 1) * 128)
            y[rows, cols] = jnp.where(lane < WIDTH, both[0], both[1]) + skip[:, cols] * wide[:, cols]

    @pl.loop(0, NCHUNK + 2)
    def _(i):
        @pl.when(i < NCHUNK)
        def _():
            ag_copy(i, 0).wait_recv()
            ag_copy(i, 3).start()
            ag_copy(i, 5).start()
            ag_copy(i, 1).wait_recv()
            ag_copy(i, 4).start()
            ag_copy(i, 6).start()

        @pl.when(i < NCHUNK - 2)
        def _():
            send_own(i + 2)

        @pl.when(i == 1)
        def _():
            @pl.loop(1, NTP)
            def _(k):
                ss_copy(k).wait_recv()

            summed = ss_recv[0]
            for k in range(1, NTP):
                summed = summed + ss_recv[k]
            r = lax.rsqrt(summed * (1.0 / MODEL) + EPSILON)
            for c in range(NCHUNK):
                rfull[c * CHUNK : (c + 1) * CHUNK, :] = jnp.broadcast_to(
                    r[c : c + 1, :], (CHUNK, 128)
                ).T

        @pl.when((i >= 1) & (i <= NCHUNK))
        def _():
            step = i - 1
            for kind in (2, 5, 6, 7, 8):
                ag_copy(step, kind).wait_recv()
            project(step)

        @pl.when(i == 1)
        def _():
            halo_send[...] = xf[ROWS : ROWS + 16, :].astype(BF16)
            halo_copy.start()

        @pl.when(i == 2)
        def _():
            halo_copy.wait_recv()
            xf[0:16, :] = jnp.where(seq > 0, halo_recv[...].astype(F32), 0.0)

        @pl.when(i >= 2)
        def _():
            scan_chunk(i - 2)

        @pl.when(i < NCHUNK)
        def _():
            ag_copy(i, 3).wait_recv()
            ag_copy(i, 7).start()
            ag_copy(i, 4).wait_recv()
            ag_copy(i, 8).start()

    logs = across_heads(total_log[...])
    high = logs.astype(BF16)
    rest = logs - high.astype(F32)
    middle = rest.astype(BF16)
    bits = [high.astype(F32), middle.astype(F32), rest - middle.astype(F32)]
    row16 = iota((16, 128), 0)
    for half in range(2):
        block = jnp.zeros((16, 128), F32)
        for part_at in range(2):
            at = half * 256 + part_at * 128
            for n in range(3):
                block = jnp.where(row16 == part_at * 8 + n, bits[n][:, at : at + 128], block)
        block = block.astype(BF16)
        for n in range(8):
            piece_send[2 * n + half, :, 0:256] = state[
                n * 16 : (n + 1) * 16, half * 256 : (half + 1) * 256
            ].astype(BF16)
            piece_send[2 * n + half, :, 256:384] = block

    def piece_copy(k):
        target = (seq + k) % NSEQ
        return pltpu.make_async_remote_copy(
            src_ref=piece_send.at[target],
            dst_ref=piece_recv.at[seq],
            send_sem=p_ssem.at[k],
            recv_sem=p_rsem.at[k],
            device_id={"seq": target},
            device_id_type=MESH,
        )

    def enter_copy(k):
        target = (seq + k) % NSEQ
        return pltpu.make_async_remote_copy(
            src_ref=enter_send.at[target],
            dst_ref=enter_recv.at[seq],
            send_sem=e_ssem.at[k],
            recv_sem=e_rsem.at[k],
            device_id={"seq": target},
            device_id_type=MESH,
        )

    @pl.loop(1, NSEQ)
    def _(k):
        piece_copy(k).start()

    piece_recv[seq] = piece_send[seq]
    carried = init_t[
        pl.ds(pl.multiple_of((seq // 2) * 16, 16), 16),
        pl.ds(pl.multiple_of((seq % 2) * 256, 256), 256),
    ]

    @pl.loop(1, NSEQ)
    def _(k):
        piece_copy(k).wait_recv()

    def combine(s, carried):
        enter_send[s] = carried.astype(BF16)
        codes = piece_recv[s, :, 256:384].astype(F32)
        log = jnp.concatenate(
            [codes[0:1] + codes[1:2] + codes[2:3], codes[8:9] + codes[9:10] + codes[10:11]], axis=1
        )
        return jnp.exp(log) * carried + piece_recv[s, :, 0:256].astype(F32)

    lax.fori_loop(0, NSEQ, combine, carried)

    @pl.loop(1, NSEQ)
    def _(k):
        enter_copy(k).start()

    enter_recv[seq] = enter_send[seq]
    loads[2].wait()

    @pl.loop(1, NSEQ)
    def _(k):
        enter_copy(k).wait_recv()

    for q in range(NSEQ):
        n, half = q // 2, q % 2
        entering[n * 16 : (n + 1) * 16, half * 256 : (half + 1) * 256] = enter_recv[q].astype(F32)

    igain_rows = igain_ref[...].astype(F32)
    igain = jnp.concatenate([igain_rows[j : j + 1, :] for j in range(4)], axis=1)

    def rs_copy(i, kind):
        src, dst, target = (
            (xs.at[i, 0], xr.at[i, 0], sibling),
            (xs.at[i, 1], xr.at[i, 1], sibling),
            (xs.at[i, 2], xr.at[i, 2], sibling),
            (xs.at[i, 3], xr.at[i, 3], sibling),
            (far_send.at[i, 0], far_recv.at[i, 0], tp_up),
            (far_send.at[i, 1], far_recv.at[i, 1], tp_down),
            (near_send.at[i, 0], near_recv.at[i, 0], tp_up),
            (near_send.at[i, 1], near_recv.at[i, 1], tp_down),
        )[kind]
        return pltpu.make_async_remote_copy(
            src_ref=src,
            dst_ref=dst,
            send_sem=rs_ssem.at[i, kind],
            recv_sem=rs_rsem.at[i, kind],
            device_id={"tp": target},
            device_id_type=MESH,
        )

    @pl.loop(0, NCHUNK + 2)
    def _(i):
        @pl.when(i < NCHUNK)
        def _():
            rows = pl.ds(pl.multiple_of(i * CHUNK, CHUNK), CHUNK)
            memory = (sloc[i] + pre[i][0:1, :] * entering[...]).astype(BF16)
            mixer = y[rows, :] + ec[rows, :] * dot(cmap[rows, :], memory)
            gated = mixer * sz[rows, :]
            scale = lax.rsqrt(jnp.mean(gated * gated, axis=1, keepdims=True) + EPSILON)
            mixed = (gated * scale * igain).astype(BF16)
            for d, z in enumerate((far, up, down, chip)):
                at = pl.multiple_of((z * 2 + 1 - core) * FEAT, FEAT)
                xs[i, d] = dot(mixed, wo[:, pl.ds(at, FEAT)]).astype(BF16)
                rs_copy(i, d).start()
            for d, z in enumerate((far, up, down, chip)):
                at = pl.multiple_of((z * 2 + core) * FEAT, FEAT)
                part[i, d] = dot(mixed, wo[:, pl.ds(at, FEAT)])
            rs_copy(i, 0).wait_recv()
            whole = (part[i, 0] + xr[i, 0].astype(F32)).astype(BF16)
            far_send[i, 0] = whole[:HALF]
            rs_copy(i, 4).start()
            far_send[i, 1] = whole[HALF:]
            rs_copy(i, 5).start()

        @pl.when((i >= 1) & (i <= NCHUNK))
        def _():
            c = i - 1
            rs_copy(c, 1).wait_recv()
            rs_copy(c, 4).wait_recv()
            whole = part[c, 1] + xr[c, 1].astype(F32)
            near_send[c, 0, 0:HALF] = (whole[:HALF] + far_recv[c, 0].astype(F32)).astype(BF16)
            near_send[c, 0, HALF:CHUNK] = whole[HALF:].astype(BF16)
            rs_copy(c, 6).start()
            rs_copy(c, 2).wait_recv()
            rs_copy(c, 5).wait_recv()
            whole = part[c, 2] + xr[c, 2].astype(F32)
            near_send[c, 1, 0:HALF] = whole[:HALF].astype(BF16)
            near_send[c, 1, HALF:CHUNK] = (whole[HALF:] + far_recv[c, 1].astype(F32)).astype(BF16)
            rs_copy(c, 7).start()

        @pl.when(i >= 2)
        def _():
            c = i - 2
            rows = pl.ds(pl.multiple_of(c * CHUNK, CHUNK), CHUNK)
            rs_copy(c, 3).wait_recv()
            summed = hidden[rows, :].astype(F32) + (part[c, 3] + xr[c, 3].astype(F32))
            rs_copy(c, 6).wait_recv()
            summed = summed + near_recv[c, 0].astype(F32)
            rs_copy(c, 7).wait_recv()
            out_ref[rows, :] = (summed + near_recv[c, 1].astype(F32)).astype(BF16)

    @pl.loop(0, NCHUNK)
    def _(i):
        for kind in range(RING_AG):
            ag_copy(i, kind).wait_send()
        for kind in range(RING_RS):
            rs_copy(i, kind).wait_send()

    @pl.loop(1, NTP)
    def _(k):
        ss_copy(k).wait_send()

    halo_copy.wait_send()

    @pl.loop(1, NSEQ)
    def _(k):
        piece_copy(k).wait_send()
        enter_copy(k).wait_send()


def on_device(
    hidden,
    norm_gain,
    gate_x_weight,
    state_weight,
    step_weight,
    conv_inner,
    conv_state,
    step_bias,
    decay_log,
    skip_gain,
    inner_gain,
    out_weight,
    initial_state,
):
    gx = gate_x_weight.reshape(MODEL, 2, 4, 128).transpose(0, 2, 1, 3).reshape(MODEL * 8, 128)
    sw = state_weight.reshape(MODEL * 2, 128)
    vmem = pl.BlockSpec(memory_space=pltpu.VMEM)
    smem = pl.BlockSpec(memory_space=pltpu.SMEM)
    anywhere = pl.BlockSpec(memory_space=pl.ANY)
    V = pltpu.VMEM
    dma = pltpu.SemaphoreType.DMA
    return pl.pallas_call(
        kernel,
        out_shape=jax.ShapeDtypeStruct((ROWS, FEAT), BF16),
        in_specs=[
            vmem, vmem, anywhere, anywhere, vmem, vmem, vmem, smem, smem, smem, vmem, anywhere, vmem,
        ],
        out_specs=vmem,
        scratch_shapes=[
            V((MODEL * 8, 128), BF16),
            V((MODEL * 2, 128), BF16),
            V((MODEL, COLS), BF16),
            V((FEAT, MODEL), BF16),
            V((ROWS, MODEL), BF16),
            V((8, 128), F32),
            V((NTP, 8, 128), F32),
            V((ROWS, 128), F32),
            V((ROWS + 16, 768), F32),
            V((8, ROWS), F32),
            V((ROWS, FEAT), F32),
            V((ROWS, FEAT), F32),
            V((ROWS, FEAT), F32),
            V((NCHUNK, STATE, FEAT), F32),
            V((NCHUNK, 8, FEAT), F32),
            V((STATE, FEAT), F32),
            V((8, 128), F32),
            V((ROWS, STATE), BF16),
            V((16, 768), BF16),
            V((16, 768), BF16),
            V((NSEQ, 16, 384), BF16),
            V((NSEQ, 16, 384), BF16),
            V((NSEQ, 16, 256), BF16),
            V((NSEQ, 16, 256), BF16),
            V((STATE, FEAT), F32),
            V((STATE, FEAT), F32),
            V((NCHUNK, 4, CHUNK, FEAT), BF16),
            V((NCHUNK, 4, CHUNK, FEAT), BF16),
            V((NCHUNK, 4, CHUNK, FEAT), F32),
            V((NCHUNK, 2, HALF, FEAT), BF16),
            V((NCHUNK, 2, CHUNK, FEAT), BF16),
            V((NCHUNK, 2, HALF, FEAT), BF16),
            V((NCHUNK, 2, CHUNK, FEAT), BF16),
            dma((3,)),
            dma((NCHUNK, RING_AG)),
            dma((NCHUNK, RING_AG)),
            dma((NTP,)),
            dma((NTP,)),
            dma,
            dma,
            dma((NSEQ,)),
            dma((NSEQ,)),
            dma((NSEQ,)),
            dma((NSEQ,)),
            dma((NCHUNK, RING_RS)),
            dma((NCHUNK, RING_RS)),
        ],
        compiler_params=pltpu.CompilerParams(
            collective_id=0, has_side_effects=True, vmem_limit_bytes=61 << 20
        ),
    )(
        hidden,
        norm_gain.reshape(MODEL // 128, 128),
        gx,
        sw,
        step_weight.T,
        conv_inner,
        conv_state.reshape(8, 128),
        step_bias,
        decay_log,
        skip_gain,
        inner_gain.reshape(4, 128),
        out_weight,
        initial_state.reshape(HEADS * WIDTH, STATE),
    )


def solution(mesh):
    return jax.shard_map(
        on_device,
        mesh=mesh,
        in_specs=(
            P("seq", "tp"),
            P(),
            P(None, None, "tp"),
            P(None, None, "tp"),
            P(None, "tp"),
            P(None, "tp"),
            P(None, None, "tp"),
            P("tp"),
            P("tp"),
            P("tp"),
            P("tp"),
            P("tp", None),
            P("tp", None, None),
        ),
        out_specs=P("seq", "tp"),
        check_vma=False,
    )
```

time: 379 us -> 93.7 us (0.25)
  waiting for transfers between devices: 164 us -> 0 us
  Pallas kernels: 0 us -> 91.7 us
  starting transfers between devices: 81.6 us -> 0 us
  matrix products: 49.7 us -> 0 us
  local copies, waits for them, and re-layouts: 51.2 us -> 1.87 us
  other arithmetic: 16.5 us -> 0 us
  between operations: 13.8 us -> 0.01 us
    pallas_call x0 -> x1, Pallas kernels: none -> 91.7 us  [on_device(): pl.pallas_call(kernel, out_shape=jax.ShapeDtypeStruct((ROWS, FEAT), BF16)...]
    ppermute x16 -> x0, starting transfers between devices: 81.6 us -> none  [from_behind(): return lax.ppermute(block, axis, route)]
    reduce_scatter x1 -> x0, waiting for transfers between devices: 78 us -> none  [on_device(): lax.psum_scatter(partial_terms, 'tp', scatter_dimension=1, tiled=True)]
    ppermute x16 -> x0, waiting for transfers between devices: 58.8 us -> none  [from_behind(): return lax.ppermute(block, axis, route)]
    dot_general x25 -> x0, matrix products: 49.7 us -> none  [the longest x4 8.54 us: block_step(): within = jnp.einsum('hts,shp->thp', scores, scaled, precision=PRECISE)]
    dynamic_update_slice x4 -> x0, local copies, waits for them, and re-layouts: 30.1 us -> none  [run_blocks(): lax.scan(block_step, (memory, start_total), (in_blocks(values), in_blocks...]
    all_gather x1 -> x0, waiting for transfers between devices: 26.4 us -> none  [on_device(): gathered = lax.all_gather(hidden, 'tp', axis=1, tiled=True)]
    unnamed x46 -> x1, local copies, waits for them, and re-layouts: 11.7 us -> 1.87 us
  transfers between devices with their start and end apart: 18 -> 0, of which waited for: 17 -> 0; matrix products, arithmetic and copies ran while one was open for 4% -> 0% of each run, Pallas kernels for 0% -> 0%
where the time goes in v2:
time: 93.7 us; the launch traced here: 93.5 us
  Pallas kernels  91.7 us (98%)
  local copies, waits for them, and re-layouts  1.87 us (2%)
    pallas_call x1, Pallas kernels, on_device(): pl.pallas_call(kernel, out_shape=jax.ShapeDtypeStruct((ROWS, FEAT), BF16)...  91.7 us

profile of v2, /device:TPU:1, one launch (start us, length us, event | category | flops | bytes accessed | tf_op | source)
XLA Modules:
  0.0 93.5 jit_solution(11453348375958260400)
XLA Ops:
  0.0 91.7 %shard_map.127 = bf16[512,512]{1,0:T(8,128)(2,1)} custom-call(bf16[512,512]{1,0:T(8,128)(2,1)} %hidden.1, bf16[32,128]{1,0:T(8,128)(2,1)} %bitcast.15, bf16[32768,128]{1,0:T(8,128)(2,1)} %bitcast.11, bf16[8192,128]{1,0:T(8,128)(2,1)} %bitcast.12, bf16[8,4096]{1,0:T(8,128)(2,1)} %bitcast.14, bf16[4,512]{1,0:T(4,128)(2,1)} %tap_x.1, bf16[8,128]{1,0:T(8,128)(2,1)} %bitcast.16, ...), custom_call_target="tpu_custom_call" | custom-call | tf_op jit(solution)/shard_map/pallas_call | solution.py:630
  91.7 1.9 %copy.16 = bf16[512,512]{1,0:T(8,128)(2,1)} copy(bf16[512,512]{1,0:T(8,128)(2,1)} %shard_map.127) | data formatting | bytes 1048576

commit v3 on v2

--- a/solution.py
+++ b/solution.py
@@ -88,6 +88,12 @@
     state,
     total_log,
     cmap,
+    vals,
+    bmap_t,
+    cols_t,
+    cum_rows,
+    step_rows,
+    mx,
     halo_send,
     halo_recv,
     piece_send,
@@ -134,8 +140,8 @@
         pltpu.make_async_copy(sw_hbm, sw_raw, load_sem.at[1]),
         pltpu.make_async_copy(wo_hbm, wo, load_sem.at[2]),
     ]
-    for load in loads:
-        load.start()
+    loads[0].start()
+    loads[1].start()
 
     barrier = pltpu.get_barrier_semaphore()
 
@@ -223,7 +229,7 @@
     o256, i256 = iota((256, 256), 0), iota((256, 256), 1)
     pick = jnp.where(i256 == (o256 % 32) * 8 + o256 // 32, 1.0, 0.0).astype(BF16)
 
-    @pl.loop(0, 64)
+    @pl.loop(0, 64, unroll=16)
     def _(b):
         at = pl.multiple_of(b * 512, 512)
         k0 = pl.multiple_of(b * 64, 64)
@@ -236,9 +242,10 @@
             w[pl.ds(k0 + 32, 32), column : column + 128] = rows[:, 128:]
 
     loads[1].wait()
+    loads[2].start()
     pick_state = jnp.where(i256 == (o256 % 128) * 2 + o256 // 128, 1.0, 0.0).astype(BF16)
 
-    @pl.loop(0, 16)
+    @pl.loop(0, 16, unroll=8)
     def _(b):
         at = pl.multiple_of(b * 512, 512)
         k0 = pl.multiple_of(b * 256, 256)
@@ -250,7 +257,7 @@
             w[pl.ds(k0, 128), column : column + 128] = rows[:, :128]
             w[pl.ds(k0 + 128, 128), column : column + 128] = rows[:, 128:]
 
-    @pl.loop(0, 32)
+    @pl.loop(0, 32, unroll=8)
     def _(b):
         at = pl.multiple_of(b * 128, 128)
         rows = stepw_ref[:, pl.ds(at, 128)].astype(F32)
@@ -289,26 +296,27 @@
         device_id_type=MESH,
     )
 
-    def project(step):
-        row = pl.multiple_of(((step + NCHUNK - 1) % NCHUNK) * CHUNK, CHUNK)
+    def chunk_of(step):
+        return (step + NCHUNK - 1) % NCHUNK
+
+    def project(c):
+        row = pl.multiple_of(c * CHUNK, CHUNK)
         rows = pl.ds(row, CHUNK)
         r = rfull[rows, :]
-        r2 = jnp.concatenate([r, r], axis=1)
-
-        @pl.loop(0, 2)
-        def _(n):
-            cols = pl.ds(pl.multiple_of(n * 256, 256), 256)
-            z = (dot(g[rows, :], w[:, cols]) * r2).astype(BF16).astype(F32)
-            sz[rows, cols] = silu(z)
-
-        @pl.loop(0, 3)
-        def _(n):
-            at = pl.multiple_of(n * 256, 256)
-            raw = (dot(g[rows, :], w[:, pl.ds(pl.multiple_of(at + 512, 256), 256)]) * r2).astype(BF16)
-            xf[pl.ds(pl.multiple_of(row + 16, 16), CHUNK), pl.ds(at, 256)] = raw.astype(F32)
-
-        raw_step = (dot(g[rows, :], w[:, 1280:1408]) * r).astype(BF16).astype(F32)
+        product = dot(g[rows, :], w[:, 512:COLS])
+        for n in range(6):
+            raw = (product[:, n * 128 : (n + 1) * 128] * r).astype(BF16).astype(F32)
+            xf[pl.ds(pl.multiple_of(row + 16, 16), CHUNK), n * 128 : (n + 1) * 128] = raw
+        raw_step = (product[:, 768:896] * r).astype(BF16).astype(F32)
         steps[:, rows] = raw_step.T[0:HEADS, :]
+
+    def project_gate(c):
+        rows = pl.ds(pl.multiple_of(c * CHUNK, CHUNK), CHUNK)
+        r = rfull[rows, :]
+        product = dot(g[rows, :], w[:, 0:512])
+        for n in range(4):
+            z = (product[:, n * 128 : (n + 1) * 128] * r).astype(BF16).astype(F32)
+            sz[rows, n * 128 : (n + 1) * 128] = silu(z)
 
     def scan_chunk(c):
         row = pl.multiple_of(c * CHUNK, CHUNK)
@@ -341,6 +349,7 @@
             for m in range(2)
         )
         cmap[rows, :] = out_map
+        vals[rows, :] = values
         in_map_t = in_map.astype(F32).T.astype(BF16)
         step = softplus(steps[:, rows] + bias)
         cum = dot(-step * rate, upper, HIGHEST)
@@ -349,11 +358,13 @@
         columns = jnp.concatenate(
             [cum, jnp.exp(cum), kept, jnp.zeros((104, 128), F32)], axis=0
         ).T
+        bmap_t[c] = in_map_t
+        cols_t[c] = columns
+        cum_rows[c] = cum
+        step_rows[c] = step
         high = columns.astype(BF16)
         low = (columns - high.astype(F32)).astype(BF16)
-        decay_exp = dot(high, spread_decay) + dot(low, spread_decay)
         step_exp = dot(high, spread_step) + dot(low, spread_step)
-        ec[rows, :] = decay_exp
         wide = values.astype(F32)
         weighted = (wide * step_exp).astype(BF16)
         before = state[...]
@@ -362,19 +373,27 @@
         total_log[...] += last
         state[...] = jnp.exp(across_heads(last)) * before + dot(in_map_t, weighted)
 
-        scores = dot(out_map, in_map_t)
+    def outputs_of(c):
+        rows = pl.ds(pl.multiple_of(c * CHUNK, CHUNK), CHUNK)
+        columns, cum, step = cols_t[c], cum_rows[c], step_rows[c]
+        high = columns.astype(BF16)
+        low = (columns - high.astype(F32)).astype(BF16)
+        ec[rows, :] = dot(high, spread_decay) + dot(low, spread_decay)
+        scores = dot(cmap[rows, :], bmap_t[c])
         lane = iota((CHUNK, 128), 1)
         for j in range(4):
-            pair = values[:, j * 128 : (j + 1) * 128]
+            cols = slice(j * 128, (j + 1) * 128)
+            pair = vals[rows, cols]
             both = []
             for h in (2 * j, 2 * j + 1):
                 spread = columns[:, h : h + 1] - cum[h : h + 1, :]
                 weights = jnp.exp(jnp.where(causal, spread, -1e30))
                 both.append(dot((scores * weights * step[h : h + 1, :]).astype(BF16), pair))
-            cols = slice(j * 128, (j + 1) * 128)
-            y[rows, cols] = jnp.where(lane < WIDTH, both[0], both[1]) + skip[:, cols] * wide[:, cols]
-
-    @pl.loop(0, NCHUNK + 2)
+            y[rows, cols] = (
+                jnp.where(lane < WIDTH, both[0], both[1]) + skip[:, cols] * pair.astype(F32)
+            )
+
+    @pl.loop(0, NCHUNK + 1)
     def _(i):
         @pl.when(i < NCHUNK)
         def _():
@@ -404,26 +423,16 @@
                     r[c : c + 1, :], (CHUNK, 128)
                 ).T
 
-        @pl.when((i >= 1) & (i <= NCHUNK))
-        def _():
-            step = i - 1
+        @pl.when(i >= 1)
+        def _():
             for kind in (2, 5, 6, 7, 8):
-                ag_copy(step, kind).wait_recv()
-            project(step)
+                ag_copy(i - 1, kind).wait_recv()
+            project(chunk_of(i - 1))
 
         @pl.when(i == 1)
         def _():
             halo_send[...] = xf[ROWS : ROWS + 16, :].astype(BF16)
             halo_copy.start()
-
-        @pl.when(i == 2)
-        def _():
-            halo_copy.wait_recv()
-            xf[0:16, :] = jnp.where(seq > 0, halo_recv[...].astype(F32), 0.0)
-
-        @pl.when(i >= 2)
-        def _():
-            scan_chunk(i - 2)
 
         @pl.when(i < NCHUNK)
         def _():
@@ -431,6 +440,25 @@
             ag_copy(i, 7).start()
             ag_copy(i, 4).wait_recv()
             ag_copy(i, 8).start()
+
+        @pl.when(i == 2)
+        def _():
+            halo_copy.wait_recv()
+            xf[0:16, :] = jnp.where(seq > 0, halo_recv[...].astype(F32), 0.0)
+
+        @pl.when(i >= 2)
+        def _():
+            scan_chunk(i - 2)
+
+        @pl.when((i >= 1) & (i < NCHUNK))
+        def _():
+            project_gate(chunk_of(i - 1))
+
+        @pl.when((i >= 2) & (i < NCHUNK))
+        def _():
+            outputs_of(i - 2)
+
+    scan_chunk(NCHUNK - 1)
 
     logs = across_heads(total_log[...])
     high = logs.astype(BF16)
@@ -478,6 +506,8 @@
         piece_copy(k).start()
 
     piece_recv[seq] = piece_send[seq]
+    project_gate(chunk_of(NCHUNK - 1))
+    outputs_of(NCHUNK - 2)
     carried = init_t[
         pl.ds(pl.multiple_of((seq // 2) * 16, 16), 16),
         pl.ds(pl.multiple_of((seq % 2) * 256, 256), 256),
@@ -487,21 +517,20 @@
     def _(k):
         piece_copy(k).wait_recv()
 
-    def combine(s, carried):
+    for s in range(NSEQ):
         enter_send[s] = carried.astype(BF16)
         codes = piece_recv[s, :, 256:384].astype(F32)
         log = jnp.concatenate(
             [codes[0:1] + codes[1:2] + codes[2:3], codes[8:9] + codes[9:10] + codes[10:11]], axis=1
         )
-        return jnp.exp(log) * carried + piece_recv[s, :, 0:256].astype(F32)
-
-    lax.fori_loop(0, NSEQ, combine, carried)
+        carried = jnp.exp(log) * carried + piece_recv[s, :, 0:256].astype(F32)
 
     @pl.loop(1, NSEQ)
     def _(k):
         enter_copy(k).start()
 
     enter_recv[seq] = enter_send[seq]
+    outputs_of(NCHUNK - 1)
     loads[2].wait()
 
     @pl.loop(1, NSEQ)
@@ -535,7 +564,17 @@
             device_id_type=MESH,
         )
 
-    @pl.loop(0, NCHUNK + 2)
+    def out_block(rows, z, to_core):
+        at = pl.multiple_of((z * 2 + to_core) * FEAT, FEAT)
+        return dot(mx[rows, :], wo[:, pl.ds(at, FEAT)])
+
+    def project_out(c, d, z):
+        rows = pl.ds(pl.multiple_of(c * CHUNK, CHUNK), CHUNK)
+        xs[c, d] = out_block(rows, z, 1 - core).astype(BF16)
+        rs_copy(c, d).start()
+        part[c, d] = out_block(rows, z, core)
+
+    @pl.loop(0, NCHUNK + 1)
     def _(i):
         @pl.when(i < NCHUNK)
         def _():
@@ -544,22 +583,27 @@
             mixer = y[rows, :] + ec[rows, :] * dot(cmap[rows, :], memory)
             gated = mixer * sz[rows, :]
             scale = lax.rsqrt(jnp.mean(gated * gated, axis=1, keepdims=True) + EPSILON)
-            mixed = (gated * scale * igain).astype(BF16)
-            for d, z in enumerate((far, up, down, chip)):
-                at = pl.multiple_of((z * 2 + 1 - core) * FEAT, FEAT)
-                xs[i, d] = dot(mixed, wo[:, pl.ds(at, FEAT)]).astype(BF16)
-                rs_copy(i, d).start()
-            for d, z in enumerate((far, up, down, chip)):
-                at = pl.multiple_of((z * 2 + core) * FEAT, FEAT)
-                part[i, d] = dot(mixed, wo[:, pl.ds(at, FEAT)])
-            rs_copy(i, 0).wait_recv()
-            whole = (part[i, 0] + xr[i, 0].astype(F32)).astype(BF16)
-            far_send[i, 0] = whole[:HALF]
-            rs_copy(i, 4).start()
-            far_send[i, 1] = whole[HALF:]
-            rs_copy(i, 5).start()
-
-        @pl.when((i >= 1) & (i <= NCHUNK))
+            mx[rows, :] = (gated * scale * igain).astype(BF16)
+            project_out(i, 0, far)
+
+        @pl.when(i >= 1)
+        def _():
+            c = i - 1
+            rs_copy(c, 0).wait_recv()
+            whole = (part[c, 0] + xr[c, 0].astype(F32)).astype(BF16)
+            far_send[c, 0] = whole[:HALF]
+            rs_copy(c, 4).start()
+            far_send[c, 1] = whole[HALF:]
+            rs_copy(c, 5).start()
+
+    @pl.loop(0, NCHUNK + 1)
+    def _(i):
+        @pl.when(i < NCHUNK)
+        def _():
+            project_out(i, 1, up)
+            project_out(i, 2, down)
+
+        @pl.when(i >= 1)
         def _():
             c = i - 1
             rs_copy(c, 1).wait_recv()
@@ -575,16 +619,19 @@
             near_send[c, 1, HALF:CHUNK] = (whole[HALF:] + far_recv[c, 1].astype(F32)).astype(BF16)
             rs_copy(c, 7).start()
 
-        @pl.when(i >= 2)
-        def _():
-            c = i - 2
-            rows = pl.ds(pl.multiple_of(c * CHUNK, CHUNK), CHUNK)
-            rs_copy(c, 3).wait_recv()
-            summed = hidden[rows, :].astype(F32) + (part[c, 3] + xr[c, 3].astype(F32))
-            rs_copy(c, 6).wait_recv()
-            summed = summed + near_recv[c, 0].astype(F32)
-            rs_copy(c, 7).wait_recv()
-            out_ref[rows, :] = (summed + near_recv[c, 1].astype(F32)).astype(BF16)
+    @pl.loop(0, NCHUNK)
+    def _(c):
+        project_out(c, 3, chip)
+
+    @pl.loop(0, NCHUNK)
+    def _(c):
+        rows = pl.ds(pl.multiple_of(c * CHUNK, CHUNK), CHUNK)
+        rs_copy(c, 3).wait_recv()
+        summed = hidden[rows, :].astype(F32) + (part[c, 3] + xr[c, 3].astype(F32))
+        rs_copy(c, 6).wait_recv()
+        summed = summed + near_recv[c, 0].astype(F32)
+        rs_copy(c, 7).wait_recv()
+        out_ref[rows, :] = (summed + near_recv[c, 1].astype(F32)).astype(BF16)
 
     @pl.loop(0, NCHUNK)
     def _(i):
@@ -653,6 +700,12 @@
             V((STATE, FEAT), F32),
             V((8, 128), F32),
             V((ROWS, STATE), BF16),
+            V((ROWS, FEAT), BF16),
+            V((NCHUNK, STATE, CHUNK), BF16),
+            V((NCHUNK, CHUNK, 128), F32),
+            V((NCHUNK, HEADS, CHUNK), F32),
+            V((NCHUNK, HEADS, CHUNK), F32),
+            V((ROWS, FEAT), BF16),
             V((16, 768), BF16),
             V((16, 768), BF16),
             V((NSEQ, 16, 384), BF16),

time: 93.7 us -> 77.7 us (0.83)
  Pallas kernels: 91.7 us -> 75.6 us
    pallas_call x1, Pallas kernels: 91.7 us -> 75.6 us  [on_device(): pl.pallas_call(kernel, out_shape=jax.ShapeDtypeStruct((ROWS, FEAT), BF16)...]
where the time goes in v3:
time: 77.7 us; the launch traced here: 77.5 us
  Pallas kernels  75.6 us (97%)
  local copies, waits for them, and re-layouts  1.87 us (2%)
    pallas_call x1, Pallas kernels, on_device(): pl.pallas_call(kernel, out_shape=jax.ShapeDtypeStruct((ROWS, FEAT), BF16)...  75.6 us
    unnamed x1, local copies, waits for them, and re-layouts  1.87 us

profile of v3, /device:TPU:1, one launch (start us, length us, event | category | flops | bytes accessed | tf_op | source)
XLA Modules:
  0.0 77.5 jit_solution(2576114220798826028)
XLA Ops:
  0.0 75.6 %shard_map.127 = bf16[512,512]{1,0:T(8,128)(2,1)} custom-call(bf16[512,512]{1,0:T(8,128)(2,1)} %hidden.1, bf16[32,128]{1,0:T(8,128)(2,1)} %bitcast.15, bf16[32768,128]{1,0:T(8,128)(2,1)} %bitcast.11, bf16[8192,128]{1,0:T(8,128)(2,1)} %bitcast.12, bf16[8,4096]{1,0:T(8,128)(2,1)} %bitcast.14, bf16[4,512]{1,0:T(4,128)(2,1)} %tap_x.1, bf16[8,128]{1,0:T(8,128)(2,1)} %bitcast.16, ...), custom_call_target="tpu_custom_call" | custom-call | tf_op jit(solution)/shard_map/pallas_call | solution.py:677
  75.6 1.9 %copy.16 = bf16[512,512]{1,0:T(8,128)(2,1)} copy(bf16[512,512]{1,0:T(8,128)(2,1)} %shard_map.127) | data formatting | bytes 1048576

commit v4 on v3

--- a/solution.py
+++ b/solution.py
@@ -223,14 +223,12 @@
         ss_copy(k).start()
 
     ss_recv[tp] = ss_send[...]
-    send_own(1)
 
     loads[0].wait()
     o256, i256 = iota((256, 256), 0), iota((256, 256), 1)
     pick = jnp.where(i256 == (o256 % 32) * 8 + o256 // 32, 1.0, 0.0).astype(BF16)
 
-    @pl.loop(0, 64, unroll=16)
-    def _(b):
+    def sort_gate_x(b):
         at = pl.multiple_of(b * 512, 512)
         k0 = pl.multiple_of(b * 64, 64)
         both = jnp.concatenate([gx_raw[pl.ds(at, 256), :], gx_raw[pl.ds(at + 256, 256), :]], axis=1)
@@ -241,6 +239,9 @@
             w[pl.ds(k0, 32), column : column + 128] = rows[:, :128]
             w[pl.ds(k0 + 32, 32), column : column + 128] = rows[:, 128:]
 
+    pl.loop(0, 32, unroll=16)(sort_gate_x)
+    send_own(1)
+    pl.loop(32, 64, unroll=16)(sort_gate_x)
     loads[1].wait()
     loads[2].start()
     pick_state = jnp.where(i256 == (o256 % 128) * 2 + o256 // 128, 1.0, 0.0).astype(BF16)
@@ -393,22 +394,9 @@
                 jnp.where(lane < WIDTH, both[0], both[1]) + skip[:, cols] * pair.astype(F32)
             )
 
-    @pl.loop(0, NCHUNK + 1)
+    @pl.loop(0, NCHUNK + 2)
     def _(i):
-        @pl.when(i < NCHUNK)
-        def _():
-            ag_copy(i, 0).wait_recv()
-            ag_copy(i, 3).start()
-            ag_copy(i, 5).start()
-            ag_copy(i, 1).wait_recv()
-            ag_copy(i, 4).start()
-            ag_copy(i, 6).start()
-
-        @pl.when(i < NCHUNK - 2)
-        def _():
-            send_own(i + 2)
-
-        @pl.when(i == 1)
+        @pl.when(i == 2)
         def _():
             @pl.loop(1, NTP)
             def _(k):
@@ -423,40 +411,49 @@
                     r[c : c + 1, :], (CHUNK, 128)
                 ).T
 
-        @pl.when(i >= 1)
+        @pl.when(i >= 2)
         def _():
             for kind in (2, 5, 6, 7, 8):
-                ag_copy(i - 1, kind).wait_recv()
-            project(chunk_of(i - 1))
-
-        @pl.when(i == 1)
+                ag_copy(i - 2, kind).wait_recv()
+            project(chunk_of(i - 2))
+
+        @pl.when(i == 2)
         def _():
             halo_send[...] = xf[ROWS : ROWS + 16, :].astype(BF16)
             halo_copy.start()
 
         @pl.when(i < NCHUNK)
         def _():
-            ag_copy(i, 3).wait_recv()
-            ag_copy(i, 7).start()
-            ag_copy(i, 4).wait_recv()
-            ag_copy(i, 8).start()
-
-        @pl.when(i == 2)
+            ag_copy(i, 0).wait_recv()
+            ag_copy(i, 3).start()
+            ag_copy(i, 5).start()
+            ag_copy(i, 1).wait_recv()
+            ag_copy(i, 4).start()
+            ag_copy(i, 6).start()
+
+        @pl.when(i < NCHUNK - 2)
+        def _():
+            send_own(i + 2)
+
+        @pl.when((i >= 1) & (i <= NCHUNK))
+        def _():
+            ag_copy(i - 1, 3).wait_recv()
+            ag_copy(i - 1, 7).start()
+            ag_copy(i - 1, 4).wait_recv()
+            ag_copy(i - 1, 8).start()
+
+        @pl.when(i == 3)
         def _():
             halo_copy.wait_recv()
             xf[0:16, :] = jnp.where(seq > 0, halo_recv[...].astype(F32), 0.0)
 
-        @pl.when(i >= 2)
-        def _():
-            scan_chunk(i - 2)
-
-        @pl.when((i >= 1) & (i < NCHUNK))
-        def _():
-            project_gate(chunk_of(i - 1))
-
-        @pl.when((i >= 2) & (i < NCHUNK))
-        def _():
-            outputs_of(i - 2)
+        @pl.when(i >= 3)
+        def _():
+            scan_chunk(i - 3)
+
+        @pl.when((i >= 2) & (i <= NCHUNK))
+        def _():
+            project_gate(chunk_of(i - 2))
 
     scan_chunk(NCHUNK - 1)
 
@@ -507,7 +504,8 @@
 
     piece_recv[seq] = piece_send[seq]
     project_gate(chunk_of(NCHUNK - 1))
-    outputs_of(NCHUNK - 2)
+    outputs_of(0)
+    outputs_of(1)
     carried = init_t[
         pl.ds(pl.multiple_of((seq // 2) * 16, 16), 16),
         pl.ds(pl.multiple_of((seq % 2) * 256, 256), 256),
@@ -530,7 +528,8 @@
         enter_copy(k).start()
 
     enter_recv[seq] = enter_send[seq]
-    outputs_of(NCHUNK - 1)
+    outputs_of(2)
+    outputs_of(3)
     loads[2].wait()
 
     @pl.loop(1, NSEQ)

time: 77.7 us -> 73.4 us (0.945)
  Pallas kernels: 75.6 us -> 71.3 us
    pallas_call x1, Pallas kernels: 75.6 us -> 71.3 us  [on_device(): pl.pallas_call(kernel, out_shape=jax.ShapeDtypeStruct((ROWS, FEAT), BF16)...]
where the time goes in v4:
time: 73.4 us; the launch traced here: 73.2 us
  Pallas kernels  71.3 us (97%)
  local copies, waits for them, and re-layouts  1.87 us (3%)
    pallas_call x1, Pallas kernels, on_device(): pl.pallas_call(kernel, out_shape=jax.ShapeDtypeStruct((ROWS, FEAT), BF16)...  71.3 us
    unnamed x1, local copies, waits for them, and re-layouts  1.87 us

profile of v4, /device:TPU:1, one launch (start us, length us, event | category | flops | bytes accessed | tf_op | source)
XLA Modules:
  0.0 73.2 jit_solution(17260863946619484956)
XLA Ops:
  0.0 71.3 %shard_map.127 = bf16[512,512]{1,0:T(8,128)(2,1)} custom-call(bf16[512,512]{1,0:T(8,128)(2,1)} %hidden.1, bf16[32,128]{1,0:T(8,128)(2,1)} %bitcast.15, bf16[32768,128]{1,0:T(8,128)(2,1)} %bitcast.11, bf16[8192,128]{1,0:T(8,128)(2,1)} %bitcast.12, bf16[8,4096]{1,0:T(8,128)(2,1)} %bitcast.14, bf16[4,512]{1,0:T(4,128)(2,1)} %tap_x.1, bf16[8,128]{1,0:T(8,128)(2,1)} %bitcast.16, ...), custom_call_target="tpu_custom_call" | custom-call | tf_op jit(solution)/shard_map/pallas_call | solution.py:676
  71.3 1.9 %copy.16 = bf16[512,512]{1,0:T(8,128)(2,1)} copy(bf16[512,512]{1,0:T(8,128)(2,1)} %shard_map.127) | data formatting | bytes 1048576

commit v5 on v4

--- a/solution.py
+++ b/solution.py
@@ -56,10 +56,22 @@
 
 
 def kernel(
+    hidden_hbm,
+    gain_hbm,
+    gx_hbm,
+    sw_hbm,
+    stepw_hbm,
+    tap_x_hbm,
+    tap_s_hbm,
+    bias_hbm,
+    decay_hbm,
+    skip_hbm,
+    igain_hbm,
+    wo_hbm,
+    init_hbm,
+    out_hbm,
     hidden,
     gain_ref,
-    gx_hbm,
-    sw_hbm,
     stepw_ref,
     tap_x,
     tap_s,
@@ -67,7 +79,6 @@
     decay_ref,
     skip_ref,
     igain_ref,
-    wo_hbm,
     init_ref,
     out_ref,
     gx_raw,
@@ -110,6 +121,7 @@
     far_recv,
     near_recv,
     load_sem,
+    out_sem,
     ag_send,
     ag_recv,
     ss_ssem,
@@ -139,11 +151,27 @@
         pltpu.make_async_copy(gx_hbm, gx_raw, load_sem.at[0]),
         pltpu.make_async_copy(sw_hbm, sw_raw, load_sem.at[1]),
         pltpu.make_async_copy(wo_hbm, wo, load_sem.at[2]),
+        pltpu.make_async_copy(hidden_hbm, hidden, load_sem.at[3]),
+        pltpu.make_async_copy(gain_hbm, gain_ref, load_sem.at[4]),
+        pltpu.make_async_copy(stepw_hbm, stepw_ref, load_sem.at[5]),
+        pltpu.make_async_copy(tap_x_hbm, tap_x, load_sem.at[6]),
+        pltpu.make_async_copy(tap_s_hbm, tap_s, load_sem.at[7]),
+        pltpu.make_async_copy(bias_hbm, bias_ref, load_sem.at[8]),
+        pltpu.make_async_copy(decay_hbm, decay_ref, load_sem.at[9]),
+        pltpu.make_async_copy(skip_hbm, skip_ref, load_sem.at[10]),
+        pltpu.make_async_copy(igain_hbm, igain_ref, load_sem.at[11]),
+        pltpu.make_async_copy(init_hbm, init_ref, load_sem.at[12]),
     ]
-    loads[0].start()
-    loads[1].start()
+    loads[3].start()
+    loads[4].start()
 
     barrier = pltpu.get_barrier_semaphore()
+
+    @pl.loop(0, NSEQ - 1)
+    def _(k):
+        pl.semaphore_signal(
+            barrier, inc=1, device_id={"seq": (seq + 1 + (k + 5) % (NSEQ - 1)) % NSEQ}, device_id_type=MESH
+        )
 
     @pl.loop(1, NTP)
     def _(k):
@@ -151,11 +179,10 @@
             barrier, inc=1, device_id={"tp": (tp + k) % NTP}, device_id_type=MESH
         )
 
-    @pl.loop(1, NSEQ)
-    def _(k):
-        pl.semaphore_signal(
-            barrier, inc=1, device_id={"seq": (seq + k) % NSEQ}, device_id_type=MESH
-        )
+    for n in (0, 1, 5, 6, 7, 8, 9, 10, 11, 12):
+        loads[n].start()
+    loads[3].wait()
+    loads[4].wait()
 
     gain_rows = gain_ref[...].astype(F32)
     gain_at = iota((MODEL // 128, 128), 0)
@@ -257,6 +284,9 @@
             rows = sorted_rows[m * 128 : (m + 1) * 128, :]
             w[pl.ds(k0, 128), column : column + 128] = rows[:, :128]
             w[pl.ds(k0 + 128, 128), column : column + 128] = rows[:, 128:]
+
+    for n in range(5, 13):
+        loads[n].wait()
 
     @pl.loop(0, 32, unroll=8)
     def _(b):
@@ -623,6 +653,28 @@
         project_out(c, 3, chip)
 
     @pl.loop(0, NCHUNK)
+    def _(i):
+        for kind in range(RING_AG):
+            ag_copy(i, kind).wait_send()
+        for kind in (0, 1, 2, 4, 5):
+            rs_copy(i, kind).wait_send()
+
+    @pl.loop(1, NTP)
+    def _(k):
+        ss_copy(k).wait_send()
+
+    halo_copy.wait_send()
+
+    @pl.loop(1, NSEQ)
+    def _(k):
+        piece_copy(k).wait_send()
+        enter_copy(k).wait_send()
+
+    def out_copy(c):
+        rows = pl.ds(pl.multiple_of(c * CHUNK, CHUNK), CHUNK)
+        return pltpu.make_async_copy(out_ref.at[rows, :], out_hbm.at[rows, :], out_sem.at[c])
+
+    @pl.loop(0, NCHUNK)
     def _(c):
         rows = pl.ds(pl.multiple_of(c * CHUNK, CHUNK), CHUNK)
         rs_copy(c, 3).wait_recv()
@@ -631,24 +683,14 @@
         summed = summed + near_recv[c, 0].astype(F32)
         rs_copy(c, 7).wait_recv()
         out_ref[rows, :] = (summed + near_recv[c, 1].astype(F32)).astype(BF16)
+        out_copy(c).start()
 
     @pl.loop(0, NCHUNK)
-    def _(i):
-        for kind in range(RING_AG):
-            ag_copy(i, kind).wait_send()
-        for kind in range(RING_RS):
-            rs_copy(i, kind).wait_send()
-
-    @pl.loop(1, NTP)
-    def _(k):
-        ss_copy(k).wait_send()
-
-    halo_copy.wait_send()
-
-    @pl.loop(1, NSEQ)
-    def _(k):
-        piece_copy(k).wait_send()
-        enter_copy(k).wait_send()
+    def _(c):
+        rs_copy(c, 3).wait_send()
+        rs_copy(c, 6).wait_send()
+        rs_copy(c, 7).wait_send()
+        out_copy(c).wait()
 
 
 def on_device(
@@ -668,19 +710,26 @@
 ):
     gx = gate_x_weight.reshape(MODEL, 2, 4, 128).transpose(0, 2, 1, 3).reshape(MODEL * 8, 128)
     sw = state_weight.reshape(MODEL * 2, 128)
-    vmem = pl.BlockSpec(memory_space=pltpu.VMEM)
-    smem = pl.BlockSpec(memory_space=pltpu.SMEM)
     anywhere = pl.BlockSpec(memory_space=pl.ANY)
     V = pltpu.VMEM
     dma = pltpu.SemaphoreType.DMA
     return pl.pallas_call(
         kernel,
         out_shape=jax.ShapeDtypeStruct((ROWS, FEAT), BF16),
-        in_specs=[
-            vmem, vmem, anywhere, anywhere, vmem, vmem, vmem, smem, smem, smem, vmem, anywhere, vmem,
-        ],
-        out_specs=vmem,
+        in_specs=[anywhere] * 13,
+        out_specs=anywhere,
         scratch_shapes=[
+            V((ROWS, FEAT), BF16),
+            V((MODEL // 128, 128), BF16),
+            V((HEADS, MODEL), BF16),
+            V((4, FEAT), BF16),
+            V((8, 128), BF16),
+            pltpu.SMEM((HEADS,), F32),
+            pltpu.SMEM((HEADS,), F32),
+            pltpu.SMEM((HEADS,), F32),
+            V((4, 128), BF16),
+            V((HEADS * WIDTH, STATE), F32),
+            V((ROWS, FEAT), BF16),
             V((MODEL * 8, 128), BF16),
             V((MODEL * 2, 128), BF16),
             V((MODEL, COLS), BF16),
@@ -720,7 +769,8 @@
             V((NCHUNK, 2, CHUNK, FEAT), BF16),
             V((NCHUNK, 2, HALF, FEAT), BF16),
             V((NCHUNK, 2, CHUNK, FEAT), BF16),
-            dma((3,)),
+            dma((13,)),
+            dma((NCHUNK,)),
             dma((NCHUNK, RING_AG)),
             dma((NCHUNK, RING_AG)),
             dma((NTP,)),

time: 73.4 us -> 71.5 us (0.974)
  Pallas kernels: 71.3 us -> 69.5 us
    pallas_call x1, Pallas kernels: 71.3 us -> 69.5 us  [on_device(): pl.pallas_call(kernel, out_shape=jax.ShapeDtypeStruct((ROWS, FEAT), BF16)...]
where the time goes in v5:
time: 71.5 us; the launch traced here: 71.4 us
  Pallas kernels  69.5 us (97%)
  local copies, waits for them, and re-layouts  1.87 us (3%)
    pallas_call x1, Pallas kernels, on_device(): pl.pallas_call(kernel, out_shape=jax.ShapeDtypeStruct((ROWS, FEAT), BF16)...  69.5 us
    unnamed x1, local copies, waits for them, and re-layouts  1.87 us

profile of v5, /device:TPU:1, one launch (start us, length us, event | category | flops | bytes accessed | tf_op | source)
XLA Modules:
  0.0 71.4 jit_solution(10642793718512438951)
XLA Ops:
  0.0 69.5 %shard_map.127 = bf16[512,512]{1,0:T(8,128)(2,1)} custom-call(bf16[512,512]{1,0:T(8,128)(2,1)} %hidden_hbm.1, bf16[32,128]{1,0:T(8,128)(2,1)} %bitcast.15, bf16[32768,128]{1,0:T(8,128)(2,1)} %bitcast.11, bf16[8192,128]{1,0:T(8,128)(2,1)} %bitcast.12, bf16[8,4096]{1,0:T(8,128)(2,1)} %bitcast.14, bf16[4,512]{1,0:T(4,128)(2,1)} %tap_x_hbm.1, ...), custom_call_target="tpu_custom_call" | custom-call | tf_op jit(solution)/shard_map/pallas_call | solution.py:716
  69.5 1.9 %copy.16 = bf16[512,512]{1,0:T(8,128)(2,1)} copy(bf16[512,512]{1,0:T(8,128)(2,1)} %shard_map.127) | data formatting | bytes 1048576

commit v6 on v5

--- a/solution.py
+++ b/solution.py
@@ -105,6 +105,7 @@
     cum_rows,
     step_rows,
     mx,
+    early,
     halo_send,
     halo_recv,
     piece_send,
@@ -330,11 +331,19 @@
     def chunk_of(step):
         return (step + NCHUNK - 1) % NCHUNK
 
+    def product_with(rows, z):
+        features = pl.ds(pl.multiple_of(z * 2 * FEAT, 2 * FEAT), 2 * FEAT)
+        return dot(g[rows, features], w[features, 512:COLS])
+
+    def project_near(c):
+        rows = pl.ds(pl.multiple_of(c * CHUNK, CHUNK), CHUNK)
+        early[...] = product_with(rows, chip) + product_with(rows, up) + product_with(rows, down)
+
     def project(c):
         row = pl.multiple_of(c * CHUNK, CHUNK)
         rows = pl.ds(row, CHUNK)
         r = rfull[rows, :]
-        product = dot(g[rows, :], w[:, 512:COLS])
+        product = early[...] + product_with(rows, far)
         for n in range(6):
             raw = (product[:, n * 128 : (n + 1) * 128] * r).astype(BF16).astype(F32)
             xf[pl.ds(pl.multiple_of(row + 16, 16), CHUNK), n * 128 : (n + 1) * 128] = raw
@@ -382,6 +391,18 @@
         cmap[rows, :] = out_map
         vals[rows, :] = values
         in_map_t = in_map.astype(F32).T.astype(BF16)
+        bmap_t[c] = in_map_t
+        last = jnp.broadcast_to(cum_rows[c][:, 127:128], (8, 128))
+        wide = values.astype(F32)
+        weighted = (wide * y[rows, :]).astype(BF16)
+        before = state[...]
+        sloc[c] = before
+        pre[c] = jnp.broadcast_to(jnp.exp(across_heads(total_log[...])), (8, FEAT))
+        total_log[...] += last
+        state[...] = jnp.exp(across_heads(last)) * before + dot(in_map_t, weighted)
+
+    def scan_steps(c):
+        rows = pl.ds(pl.multiple_of(c * CHUNK, CHUNK), CHUNK)
         step = softplus(steps[:, rows] + bias)
         cum = dot(-step * rate, upper, HIGHEST)
         last = jnp.broadcast_to(cum[:, 127:128], (8, 128))
@@ -389,20 +410,13 @@
         columns = jnp.concatenate(
             [cum, jnp.exp(cum), kept, jnp.zeros((104, 128), F32)], axis=0
         ).T
-        bmap_t[c] = in_map_t
         cols_t[c] = columns
         cum_rows[c] = cum
         step_rows[c] = step
         high = columns.astype(BF16)
         low = (columns - high.astype(F32)).astype(BF16)
         step_exp = dot(high, spread_step) + dot(low, spread_step)
-        wide = values.astype(F32)
-        weighted = (wide * step_exp).astype(BF16)
-        before = state[...]
-        sloc[c] = before
-        pre[c] = jnp.broadcast_to(jnp.exp(across_heads(total_log[...])), (8, FEAT))
-        total_log[...] += last
-        state[...] = jnp.exp(across_heads(last)) * before + dot(in_map_t, weighted)
+        y[rows, :] = step_exp
 
     def outputs_of(c):
         rows = pl.ds(pl.multiple_of(c * CHUNK, CHUNK), CHUNK)
@@ -443,9 +457,10 @@
 
         @pl.when(i >= 2)
         def _():
-            for kind in (2, 5, 6, 7, 8):
+            for kind in (7, 8):
                 ag_copy(i - 2, kind).wait_recv()
             project(chunk_of(i - 2))
+            scan_steps(chunk_of(i - 2))
 
         @pl.when(i == 2)
         def _():
@@ -467,6 +482,9 @@
 
         @pl.when((i >= 1) & (i <= NCHUNK))
         def _():
+            for kind in (2, 5, 6):
+                ag_copy(i - 1, kind).wait_recv()
+            project_near(chunk_of(i - 1))
             ag_copy(i - 1, 3).wait_recv()
             ag_copy(i - 1, 7).start()
             ag_copy(i - 1, 4).wait_recv()
@@ -480,10 +498,6 @@
         @pl.when(i >= 3)
         def _():
             scan_chunk(i - 3)
-
-        @pl.when((i >= 2) & (i <= NCHUNK))
-        def _():
-            project_gate(chunk_of(i - 2))
 
     scan_chunk(NCHUNK - 1)
 
@@ -533,9 +547,12 @@
         piece_copy(k).start()
 
     piece_recv[seq] = piece_send[seq]
-    project_gate(chunk_of(NCHUNK - 1))
-    outputs_of(0)
-    outputs_of(1)
+
+    @pl.loop(0, 2)
+    def _(c):
+        project_gate(c)
+        outputs_of(c)
+
     carried = init_t[
         pl.ds(pl.multiple_of((seq // 2) * 16, 16), 16),
         pl.ds(pl.multiple_of((seq % 2) * 256, 256), 256),
@@ -558,8 +575,12 @@
         enter_copy(k).start()
 
     enter_recv[seq] = enter_send[seq]
-    outputs_of(2)
-    outputs_of(3)
+
+    @pl.loop(2, 4)
+    def _(c):
+        project_gate(c)
+        outputs_of(c)
+
     loads[2].wait()
 
     @pl.loop(1, NSEQ)
@@ -625,28 +646,22 @@
             far_send[c, 1] = whole[HALF:]
             rs_copy(c, 5).start()
 
-    @pl.loop(0, NCHUNK + 1)
-    def _(i):
-        @pl.when(i < NCHUNK)
-        def _():
-            project_out(i, 1, up)
-            project_out(i, 2, down)
-
-        @pl.when(i >= 1)
-        def _():
-            c = i - 1
-            rs_copy(c, 1).wait_recv()
-            rs_copy(c, 4).wait_recv()
-            whole = part[c, 1] + xr[c, 1].astype(F32)
-            near_send[c, 0, 0:HALF] = (whole[:HALF] + far_recv[c, 0].astype(F32)).astype(BF16)
-            near_send[c, 0, HALF:CHUNK] = whole[HALF:].astype(BF16)
-            rs_copy(c, 6).start()
-            rs_copy(c, 2).wait_recv()
-            rs_copy(c, 5).wait_recv()
-            whole = part[c, 2] + xr[c, 2].astype(F32)
-            near_send[c, 1, 0:HALF] = whole[:HALF].astype(BF16)
-            near_send[c, 1, HALF:CHUNK] = (whole[HALF:] + far_recv[c, 1].astype(F32)).astype(BF16)
-            rs_copy(c, 7).start()
+    @pl.loop(0, NCHUNK)
+    def _(c):
+        project_out(c, 1, up)
+        project_out(c, 2, down)
+        rs_copy(c, 1).wait_recv()
+        rs_copy(c, 4).wait_recv()
+        whole = part[c, 1] + xr[c, 1].astype(F32)
+        near_send[c, 0, 0:HALF] = (whole[:HALF] + far_recv[c, 0].astype(F32)).astype(BF16)
+        near_send[c, 0, HALF:CHUNK] = whole[HALF:].astype(BF16)
+        rs_copy(c, 6).start()
+        rs_copy(c, 2).wait_recv()
+        rs_copy(c, 5).wait_recv()
+        whole = part[c, 2] + xr[c, 2].astype(F32)
+        near_send[c, 1, 0:HALF] = whole[:HALF].astype(BF16)
+        near_send[c, 1, HALF:CHUNK] = (whole[HALF:] + far_recv[c, 1].astype(F32)).astype(BF16)
+        rs_copy(c, 7).start()
 
     @pl.loop(0, NCHUNK)
     def _(c):
@@ -670,17 +685,21 @@
         piece_copy(k).wait_send()
         enter_copy(k).wait_send()
 
-    def out_copy(c):
-        rows = pl.ds(pl.multiple_of(c * CHUNK, CHUNK), CHUNK)
-        return pltpu.make_async_copy(out_ref.at[rows, :], out_hbm.at[rows, :], out_sem.at[c])
-
     @pl.loop(0, NCHUNK)
     def _(c):
         rows = pl.ds(pl.multiple_of(c * CHUNK, CHUNK), CHUNK)
         rs_copy(c, 3).wait_recv()
-        summed = hidden[rows, :].astype(F32) + (part[c, 3] + xr[c, 3].astype(F32))
+        part[c, 3] = hidden[rows, :].astype(F32) + (part[c, 3] + xr[c, 3].astype(F32))
+
+    def out_copy(c):
+        rows = pl.ds(pl.multiple_of(c * CHUNK, CHUNK), CHUNK)
+        return pltpu.make_async_copy(out_ref.at[rows, :], out_hbm.at[rows, :], out_sem.at[c])
+
+    @pl.loop(0, NCHUNK)
+    def _(c):
+        rows = pl.ds(pl.multiple_of(c * CHUNK, CHUNK), CHUNK)
         rs_copy(c, 6).wait_recv()
-        summed = summed + near_recv[c, 0].astype(F32)
+        summed = part[c, 3] + near_recv[c, 0].astype(F32)
         rs_copy(c, 7).wait_recv()
         out_ref[rows, :] = (summed + near_recv[c, 1].astype(F32)).astype(BF16)
         out_copy(c).start()
@@ -754,6 +773,7 @@
             V((NCHUNK, HEADS, CHUNK), F32),
             V((NCHUNK, HEADS, CHUNK), F32),
             V((ROWS, FEAT), BF16),
+            V((CHUNK, COLS - 512), F32),
             V((16, 768), BF16),
             V((16, 768), BF16),
             V((NSEQ, 16, 384), BF16),

time: 71.5 us -> 70 us (0.979)
  Pallas kernels: 69.5 us -> 68 us
    pallas_call x1, Pallas kernels: 69.5 us -> 68 us  [on_device(): pl.pallas_call(kernel, out_shape=jax.ShapeDtypeStruct((ROWS, FEAT), BF16)...]
where the time goes in v6:
time: 70 us; the launch traced here: 69.8 us
  Pallas kernels  68 us (97%)
  local copies, waits for them, and re-layouts  1.87 us (3%)
    pallas_call x1, Pallas kernels, on_device(): pl.pallas_call(kernel, out_shape=jax.ShapeDtypeStruct((ROWS, FEAT), BF16)...  68 us
    unnamed x1, local copies, waits for them, and re-layouts  1.87 us

profile of v6, /device:TPU:1, one launch (start us, length us, event | category | flops | bytes accessed | tf_op | source)
XLA Modules:
  0.0 69.8 jit_solution(2344051591741529793)
XLA Ops:
  0.0 68.0 %shard_map.127 = bf16[512,512]{1,0:T(8,128)(2,1)} custom-call(bf16[512,512]{1,0:T(8,128)(2,1)} %hidden_hbm.1, bf16[32,128]{1,0:T(8,128)(2,1)} %bitcast.15, bf16[32768,128]{1,0:T(8,128)(2,1)} %bitcast.11, bf16[8192,128]{1,0:T(8,128)(2,1)} %bitcast.12, bf16[8,4096]{1,0:T(8,128)(2,1)} %bitcast.14, bf16[4,512]{1,0:T(4,128)(2,1)} %tap_x_hbm.1, ...), custom_call_target="tpu_custom_call" | custom-call | tf_op jit(solution)/shard_map/pallas_call | solution.py:735
  68.0 1.9 %copy.16 = bf16[512,512]{1,0:T(8,128)(2,1)} copy(bf16[512,512]{1,0:T(8,128)(2,1)} %shard_map.127) | data formatting | bytes 1048576

commit v7 on v6

--- a/solution.py
+++ b/solution.py
@@ -438,7 +438,7 @@
                 jnp.where(lane < WIDTH, both[0], both[1]) + skip[:, cols] * pair.astype(F32)
             )
 
-    @pl.loop(0, NCHUNK + 2)
+    @pl.loop(0, NCHUNK + 1)
     def _(i):
         @pl.when(i == 2)
         def _():
@@ -499,6 +499,11 @@
         def _():
             scan_chunk(i - 3)
 
+    for kind in (7, 8):
+        ag_copy(NCHUNK - 1, kind).wait_recv()
+    project(NCHUNK - 2)
+    scan_steps(NCHUNK - 2)
+    scan_chunk(NCHUNK - 2)
     scan_chunk(NCHUNK - 1)
 
     logs = across_heads(total_log[...])
@@ -521,7 +526,7 @@
             piece_send[2 * n + half, :, 256:384] = block
 
     def piece_copy(k):
-        target = (seq + k) % NSEQ
+        target = (seq + 1 + (k + 4) % (NSEQ - 1)) % NSEQ
         return pltpu.make_async_remote_copy(
             src_ref=piece_send.at[target],
             dst_ref=piece_recv.at[seq],
@@ -532,7 +537,7 @@
         )
 
     def enter_copy(k):
-        target = (seq + k) % NSEQ
+        target = (seq + 1 + (k + 4) % (NSEQ - 1)) % NSEQ
         return pltpu.make_async_remote_copy(
             src_ref=enter_send.at[target],
             dst_ref=enter_recv.at[seq],

time: 70 us -> 69.1 us (0.987)
  Pallas kernels: 68 us -> 67 us
    pallas_call x1, Pallas kernels: 68 us -> 67 us  [on_device(): pl.pallas_call(kernel, out_shape=jax.ShapeDtypeStruct((ROWS, FEAT), BF16)...]
where the time goes in v7:
time: 69.1 us; the launch traced here: 68.9 us
  Pallas kernels  67 us (97%)
  local copies, waits for them, and re-layouts  1.87 us (3%)
    pallas_call x1, Pallas kernels, on_device(): pl.pallas_call(kernel, out_shape=jax.ShapeDtypeStruct((ROWS, FEAT), BF16)...  67 us
    unnamed x1, local copies, waits for them, and re-layouts  1.87 us

profile of v7, /device:TPU:1, one launch (start us, length us, event | category | flops | bytes accessed | tf_op | source)
XLA Modules:
  0.0 68.9 jit_solution(3176353427218206429)
XLA Ops:
  0.0 67.0 %shard_map.127 = bf16[512,512]{1,0:T(8,128)(2,1)} custom-call(bf16[512,512]{1,0:T(8,128)(2,1)} %hidden_hbm.1, bf16[32,128]{1,0:T(8,128)(2,1)} %bitcast.15, bf16[32768,128]{1,0:T(8,128)(2,1)} %bitcast.11, bf16[8192,128]{1,0:T(8,128)(2,1)} %bitcast.12, bf16[8,4096]{1,0:T(8,128)(2,1)} %bitcast.14, bf16[4,512]{1,0:T(4,128)(2,1)} %tap_x_hbm.1, ...), custom_call_target="tpu_custom_call" | custom-call | tf_op jit(solution)/shard_map/pallas_call | solution.py:740
  67.0 1.9 %copy.16 = bf16[512,512]{1,0:T(8,128)(2,1)} copy(bf16[512,512]{1,0:T(8,128)(2,1)} %shard_map.127) | data formatting | bytes 1048576

commit v8 on v7

--- a/solution.py
+++ b/solution.py
@@ -575,9 +575,9 @@
         )
         carried = jnp.exp(log) * carried + piece_recv[s, :, 0:256].astype(F32)
 
-    @pl.loop(1, NSEQ)
-    def _(k):
-        enter_copy(k).start()
+        @pl.when(seq != s)
+        def _():
+            enter_copy(((s + NSEQ - seq) % NSEQ + 9) % (NSEQ - 1) + 1).start()
 
     enter_recv[seq] = enter_send[seq]
 

time: 69.1 us -> 68.5 us (level)
  no operation moved by 1% of the time
where the time goes in v8:
time: 68.5 us; the launch traced here: 68.3 us
  Pallas kernels  66.4 us (97%)
  local copies, waits for them, and re-layouts  1.87 us (3%)
    pallas_call x1, Pallas kernels, on_device(): pl.pallas_call(kernel, out_shape=jax.ShapeDtypeStruct((ROWS, FEAT), BF16)...  66.4 us
    unnamed x1, local copies, waits for them, and re-layouts  1.87 us

profile of v8, /device:TPU:1, one launch (start us, length us, event | category | flops | bytes accessed | tf_op | source)
XLA Modules:
  0.0 68.3 jit_solution(3400479632687066285)
XLA Ops:
  0.0 66.4 %shard_map.127 = bf16[512,512]{1,0:T(8,128)(2,1)} custom-call(bf16[512,512]{1,0:T(8,128)(2,1)} %hidden_hbm.1, bf16[32,128]{1,0:T(8,128)(2,1)} %bitcast.15, bf16[32768,128]{1,0:T(8,128)(2,1)} %bitcast.11, bf16[8192,128]{1,0:T(8,128)(2,1)} %bitcast.12, bf16[8,4096]{1,0:T(8,128)(2,1)} %bitcast.14, bf16[4,512]{1,0:T(4,128)(2,1)} %tap_x_hbm.1, ...), custom_call_target="tpu_custom_call" | custom-call | tf_op jit(solution)/shard_map/pallas_call | solution.py:740
  66.4 1.9 %copy.16 = bf16[512,512]{1,0:T(8,128)(2,1)} copy(bf16[512,512]{1,0:T(8,128)(2,1)} %shard_map.127) | data formatting | bytes 1048576
